TPU v7x, 256 devices: a whole 4x4x8 slice. The times are simulated.
256 devices in a mesh: gx: 32 (over z_lo, y, core), gy: 8 (over x, z_hi).
Axes of the slice: x: 4, y: 4, z: 8 (z_hi: 2, z_lo: 4; z = z_hi * 4 + z_lo), core: 2. Of those that a mesh axis runs over, the one named last changes fastest.
Arguments:
- features: bfloat16 [512, 512, 128], P(('gx', 'gy')), may hold values from -6 to 6
- occupied: int32 [512, 512], P(('gx', 'gy')), may hold values 0 or 1
- weight_one: bfloat16 [27, 128, 128], replicated, may hold values from -0.109375 to 0.109375
- bias_one: float32 [128], replicated, may hold values from -3 to 3
- weight_two: bfloat16 [27, 128, 128], replicated, may hold values from -0.109375 to 0.109375
- cotangent: bfloat16 [512, 512, 128], P(('gx', 'gy')), may hold values from -6 to 6
- neighbours: int32 [512, 27], P(('gx', 'gy')), may hold values from 0 to 18, as said below
- send_x: int32 [256, 2, 6], P(('gx', 'gy')), may hold values from 0 to 18, as said below
- send_y: int32 [256, 2, 2], P(('gx', 'gy')), may hold values from 0 to 18, as said below
Outputs:
- output: bfloat16 [512, 512, 128], P(('gx', 'gy'))
- grad_features: bfloat16 [512, 512, 128], P(('gx', 'gy'))
- grad_weight_one: float32 [27, 128, 128], replicated
- grad_weight_two: float32 [27, 128, 128], replicated
Inputs may be any that keep to these rules, and one draw needn't show every extreme that they name: `neighbours`: each tile is 2 x 2 x 2 bricks of the map, tiles laid out with x over gx and y over gy. A tile's live bricks fill its first slots, and some tile is full in every draw. A live brick's entry k names the pool row holding the brick at brick offset (k // 9 - 1, k // 3 % 3 - 1, k % 3 - 1), or 18 where that brick is empty or lies outside the map; entry 13 names its own slot; a dead slot's entries are all 18. The lists describe one map, so neighbourhood is symmetric. send_y[t, 0] lists in slot order the live slots of tile t in its top layer of bricks along y, send_y[t, 1] those in its bottom layer; the rest is 18. send_x[t, 0] lists in row order the pool rows below 6 of tile t (its own bricks and those it received along y) whose bricks lie in its top layer along x, send_x[t, 1] those in its bottom layer; the rest is 18.
All inputs are finite; a program needn't handle non-finite values. No bound on the sum of `occupied` on one device may be relied on, other than what follows from the above.
Results may differ from a plain program's by a relative error of at most 0.015.
Values may be sent and summed in bfloat16 or wider, within the bound.
A program may use at most 128 MiB of HBM per device.

v0:
```python
import math

import jax
import jax.numpy as jnp
from jax import lax
from jax.sharding import PartitionSpec as P

EDGE = 8
KVOL = 27


def shifted(block, axis, distance):
    devices = range(lax.axis_size(axis))
    route = [(i - distance, i) for i in devices if i - distance in devices]
    return lax.ppermute(block, axis, route)


def cut_layer(portion, side_code, along_axis):
    extent = portion.shape[along_axis]
    if side_code == 0:
        return lax.slice_in_dim(portion, extent - 1, extent, axis=along_axis)
    if side_code == 2:
        return lax.slice_in_dim(portion, 0, 1, axis=along_axis)
    return portion


def pick_rows(bricks, row_index):
    row_count = bricks.shape[0]
    clipped = jnp.where(row_index < row_count, row_index, row_count)
    padded_rows = jnp.concatenate([bricks, jnp.zeros((1,) + bricks.shape[1:], bricks.dtype)], 0)
    return padded_rows[clipped]


def fill_pool(voxel_field, send_x, send_y, brick_edge):
    slots, voxels, channels = voxel_field.shape
    bricks = voxel_field.reshape(slots, brick_edge, brick_edge, brick_edge, channels)
    gathered = [bricks]
    for lane_idx, shift_by, side_code in ((0, 1, 0), (1, -1, 2)):
        chosen = pick_rows(bricks, send_y[0, lane_idx])
        arrived = shifted(chosen, "gy", shift_by)
        gathered.append(arrived)
    first_section = jnp.concatenate(gathered, 0)
    pooled = [first_section]
    for lane_idx, shift_by, side_code in ((0, 1, 0), (1, -1, 2)):
        chosen = pick_rows(first_section, send_x[0, lane_idx])
        arrived = shifted(chosen, "gx", shift_by)
        pooled.append(arrived)
    pooled.append(jnp.zeros((1,) + bricks.shape[1:], bricks.dtype))
    return jnp.concatenate(pooled, 0)


def gather_block(pool_rows, neighbours):
    layers_x = []
    for off_x in range(3):
        layers_y = []
        for off_y in range(3):
            layers_z = []
            for off_z in range(3):
                portion = cut_layer(cut_layer(cut_layer(pool_rows, off_x, 1), off_y, 2), off_z, 3)
                layers_z.append(portion[neighbours[:, 9 * off_x + 3 * off_y + off_z]])
            layers_y.append(jnp.concatenate(layers_z, axis=3))
        layers_x.append(jnp.concatenate(layers_y, axis=2))
    return jnp.concatenate(layers_x, axis=1)


def to_columns(padded_block, brick_edge):
    tap_list = []
    for off_x in range(3):
        for off_y in range(3):
            for off_z in range(3):
                tap_list.append(
                    padded_block[
                        :,
                        off_x : off_x + brick_edge,
                        off_y : off_y + brick_edge,
                        off_z : off_z + brick_edge,
                    ]
                )
    stacked = jnp.stack(tap_list, axis=4)
    return stacked.reshape(-1, len(tap_list) * padded_block.shape[-1])


def transpose_conv(grad_field, weight, neighbours, send_x, send_y, brick_edge):
    slots, voxels, channels = grad_field.shape
    flipped = jnp.flip(weight, 0).transpose(0, 2, 1).reshape(-1, channels)
    pool_rows = fill_pool(grad_field, send_x, send_y, brick_edge)
    columns = to_columns(gather_block(pool_rows, neighbours), brick_edge)
    result = jnp.dot(columns, flipped, preferred_element_type=jnp.float32)
    return result.reshape(slots, voxels, channels)


def on_device(
    features, occupied, weight_one, bias_one, weight_two, cotangent, neighbours, send_x, send_y
):
    slots, voxels, channels = features.shape
    brick_edge = EDGE
    pool_end = slots + 2 * send_y.shape[2] + 2 * send_x.shape[2]
    live_bricks = (neighbours[:, 13] != pool_end).astype(jnp.int32)
    voxel_mask = (occupied * live_bricks[:, None]).astype(jnp.float32)[:, :, None]
    mask_half = voxel_mask.astype(jnp.bfloat16)
    masked = features * mask_half
    flat_one = weight_one.reshape(KVOL * channels, channels)
    flat_two = weight_two.reshape(KVOL * channels, channels)
    cols_input = to_columns(
        gather_block(fill_pool(masked, send_x, send_y, brick_edge), neighbours), brick_edge
    )
    preact = (
        jnp.dot(cols_input, flat_one, preferred_element_type=jnp.float32).reshape(
            slots, voxels, channels
        )
        + bias_one
    )
    hidden = (jax.nn.relu(preact) * voxel_mask).astype(jnp.bfloat16)
    cols_hidden = to_columns(
        gather_block(fill_pool(hidden, send_x, send_y, brick_edge), neighbours), brick_edge
    )
    second_conv = jnp.dot(cols_hidden, flat_two, preferred_element_type=jnp.float32).reshape(
        slots, voxels, channels
    )
    output = (second_conv * voxel_mask + masked.astype(jnp.float32)).astype(jnp.bfloat16)
    grad_out = cotangent * mask_half
    back_two = transpose_conv(grad_out, weight_two, neighbours, send_x, send_y, brick_edge)
    contract = (((0,), (0,)), ((), ()))
    sum_two = lax.dot_general(
        cols_hidden,
        grad_out.reshape(slots * voxels, channels),
        contract,
        preferred_element_type=jnp.float32,
    )
    grad_hidden = jnp.where(preact > 0, back_two * voxel_mask, 0.0).astype(jnp.bfloat16)
    back_one = transpose_conv(grad_hidden, weight_one, neighbours, send_x, send_y, brick_edge)
    sum_one = lax.dot_general(
        cols_input,
        grad_hidden.reshape(slots * voxels, channels),
        contract,
        preferred_element_type=jnp.float32,
    )
    sum_one, sum_two = lax.psum((sum_one, sum_two), ("gx", "gy"))
    grad_scale = 1.0 / math.sqrt(slots * voxels * lax.axis_size("gx") * lax.axis_size("gy"))
    grad_features = ((cotangent.astype(jnp.float32) + back_one) * voxel_mask).astype(jnp.bfloat16)
    grad_weight_one = (sum_one * grad_scale).reshape(KVOL, channels, channels)
    grad_weight_two = (sum_two * grad_scale).reshape(KVOL, channels, channels)
    return (output, grad_features, grad_weight_one, grad_weight_two)


def solution(mesh):
    in_specs = (
        P(("gx", "gy"), None, None),
        P(("gx", "gy"), None),
        P(),
        P(),
        P(),
        P(("gx", "gy"), None, None),
        P(("gx", "gy"), None),
        P(("gx", "gy"), None, None),
        P(("gx", "gy"), None, None),
    )
    out_specs = (P(("gx", "gy"), None, None), P(("gx", "gy"), None, None), P(), P())
    return jax.shard_map(
        on_device, mesh=mesh, in_specs=in_specs, out_specs=out_specs, check_vma=False
    )
```

profile of v0, /device:TPU:1, one launch (start us, length us, event | category | flops | bytes accessed | tf_op | source)
XLA Modules:
  0.0 848.5 jit_solution(8771616513204699121)
XLA Ops:
  13.2 9.6 %collective-permute-start = (bf16[2,8,8,8,128]{4,3,2,1,0:T(8,128)(2,1)}, bf16[2,8,8,8,128]{4,3,2,1,0:T(8,128)(2,1)S(1)}, u32[]{:S(2)}, u32[]{:S(2)}) collective-permute-start(bf16[2,8,8,8,128]{4,3,2,1,0:T(8,128)(2,1)} %gather_fusion), channel_id=1, source_target_pairs={{0,1},{1,2},{2,3},{3,4},{4,5},{5,6},{6,7},{8,9},{9,10},{10,11},{11... | collective-permute-start | bytes 786440 | tf_op jit(solution)/shard_map/ppermute | solution.py:15
  26.7 7.9 collective-permute-start.8
  50.9 8.3 collective-permute-done.9
  61.4 4.4 collective-permute-start.2
  73.9 3.6 collective-permute-start.10
  249.5 4.1 copy.248
  275.6 4.7 copy.198
  280.4 4.6 multiply_convert_fusion
  293.1 17.6 %collective-permute-start.12 = (bf16[2,8,8,8,128]{4,3,2,1,0:T(8,128)(2,1)}, bf16[2,8,8,8,128]{4,3,2,1,0:T(8,128)(2,1)S(1)}, u32[]{:S(2)}, u32[]{:S(2)}) collective-permute-start(bf16[2,8,8,8,128]{4,3,2,1,0:T(8,128)(2,1)} %gather_fusion.93), channel_id=1, source_target_pairs={{0,1},{1,2},{2,3},{3,4},{4,5},{5,6},{6,7},{8,9},{9,10},{10,11},{11... | collective-permute-start | bytes 786440 | tf_op jit(solution)/shard_map/ppermute | solution.py:15
  312.0 7.9 collective-permute-start.4
  323.5 11.5 %collective-permute-done.13 = bf16[2,8,8,8,128]{4,3,2,1,0:T(8,128)(2,1)S(1)} collective-permute-done((bf16[2,8,8,8,128]{4,3,2,1,0:T(8,128)(2,1)}, bf16[2,8,8,8,128]{4,3,2,1,0:T(8,128)(2,1)S(1)}, u32[]{:S(2)}, u32[]{:S(2)}) %collective-permute-start.13) | collective-permute-done | bytes 262176 | tf_op jit(solution)/shard_map/ppermute | solution.py:15
  335.0 11.3 %collective-permute-done.5 = bf16[2,8,8,8,128]{4,3,2,1,0:T(8,128)(2,1)} collective-permute-done((bf16[2,8,8,8,128]{4,3,2,1,0:T(8,128)(2,1)}, bf16[2,8,8,8,128]{4,3,2,1,0:T(8,128)(2,1)}, u32[]{:S(2)}, u32[]{:S(2)}) %collective-permute-start.5) | collective-permute-done | bytes 262176 | tf_op jit(solution)/shard_map/ppermute | solution.py:15
  349.2 2.7 collective-permute-start.6
  352.0 6.3 fusion.65
  367.3 3.1 collective-permute-start.14
  395.4 4.9 fusion.58
  548.9 4.2 copy.223
  553.1 2.8 copy-done.1
  556.0 3.3 fusion.66
  561.6 4.7 copy.274
  566.4 4.0 fusion.5
  570.4 2.7 fusion.4
  573.1 264.1 %all-reduce.7.cloned.1.call-done = (f32[3456,128]{1,0:T(8,128)}, f32[3456,128]{1,0:T(8,128)}) async-done(((f32[3456,128]{1,0:T(8,128)}, f32[3456,128]{1,0:T(8,128)}), (f32[3456,128]{1,0:T(8,128)}, f32[3456,128]{1,0:T(8,128)})) %all-reduce.7.cloned.1.call-update) | async-done | bytes 3538960 | tf_op jit(solution)/shard_map/psum | solution.py:138
  837.2 2.9 broadcast_multiply_fusion.1
  (737 shorter events, 430.7 us)
Async XLA Ops:
  7.2 830.0 %all-reduce.7.cloned.1.call-start = ((), (), s32[]{:S(2)}) async-start(), calls=%async_computation | async-start | bytes 7077888 | tf_op jit(solution)/shard_map/psum | solution.py:138
  11.8 47.4 %copy-start.6 = (bf16[2,512,128]{2,1,0:T(8,128)(2,1)}, bf16[2,512,128]{2,1,0:T(8,128)(2,1)S(1)}, u32[]{:S(2)}) copy-start(bf16[2,512,128]{2,1,0:T(8,128)(2,1)S(1)} %get-tuple-element.125) | copy-start | bytes 786436
  13.2 37.7 %collective-permute-start = (bf16[2,8,8,8,128]{4,3,2,1,0:T(8,128)(2,1)}, bf16[2,8,8,8,128]{4,3,2,1,0:T(8,128)(2,1)S(1)}, u32[]{:S(2)}, u32[]{:S(2)}) collective-permute-start(bf16[2,8,8,8,128]{4,3,2,1,0:T(8,128)(2,1)} %gather_fusion), channel_id=1, source_target_pairs={{0,1},{1,2},{2,3},{3,4},{4,5},{5,6},{6,7},{8,9},{9,10},{10,11},{11... | collective-permute-start | bytes 786440 | tf_op jit(solution)/shard_map/ppermute | solution.py:15
  24.1 26.7 %collective-permute-start.1 = (bf16[2,8,8,8,128]{4,3,2,1,0:T(8,128)(2,1)}, bf16[2,8,8,8,128]{4,3,2,1,0:T(8,128)(2,1)S(1)}, u32[]{:S(2)}, u32[]{:S(2)}) collective-permute-start(bf16[2,8,8,8,128]{4,3,2,1,0:T(8,128)(2,1)} %gather_fusion.1), channel_id=1, source_target_pairs={{1,0},{2,1},{3,2},{4,3},{5,4},{6,5},{7,6},{9,8},{10,9},{11,10},{12... | collective-permute-start | bytes 786440 | tf_op jit(solution)/shard_map/ppermute | solution.py:15
  26.7 24.1 %collective-permute-start.8 = (bf16[2,8,8,8,128]{4,3,2,1,0:T(8,128)(2,1)}, bf16[2,8,8,8,128]{4,3,2,1,0:T(8,128)(2,1)S(1)}, u32[]{:S(2)}, u32[]{:S(2)}) collective-permute-start(bf16[2,8,8,8,128]{4,3,2,1,0:T(8,128)(2,1)} %gather_fusion.62), channel_id=1, source_target_pairs={{0,1},{1,2},{2,3},{3,4},{4,5},{5,6},{6,7},{8,9},{9,10},{10,11},{11... | collective-permute-start | bytes 786440 | tf_op jit(solution)/shard_map/ppermute | solution.py:15
  35.9 23.2 %collective-permute-start.9 = (bf16[2,8,8,8,128]{4,3,2,1,0:T(8,128)(2,1)}, bf16[2,8,8,8,128]{4,3,2,1,0:T(8,128)(2,1)S(1)}, u32[]{:S(2)}, u32[]{:S(2)}) collective-permute-start(bf16[2,8,8,8,128]{4,3,2,1,0:T(8,128)(2,1)} %gather_fusion.63), channel_id=1, source_target_pairs={{1,0},{2,1},{3,2},{4,3},{5,4},{6,5},{7,6},{9,8},{10,9},{11,10},{12... | collective-permute-start | bytes 786440 | tf_op jit(solution)/shard_map/ppermute | solution.py:15
  42.5 100.4 %copy-start.65 = (s32[1024]{0:T(1024)}, s32[1024]{0:T(1024)S(1)}, u32[]{:S(2)}) copy-start(s32[1024]{0:T(1024)S(1)} %get-tuple-element.180) | copy-start | bytes 12292
  61.4 21.2 %collective-permute-start.2 = (bf16[6,8,8,8,128]{4,3,2,1,0:T(8,128)(2,1)}, bf16[6,8,8,8,128]{4,3,2,1,0:T(8,128)(2,1)}, u32[]{:S(2)}, u32[]{:S(2)}) collective-permute-start(bf16[6,8,8,8,128]{4,3,2,1,0:T(8,128)(2,1)} %gather_fusion.2), channel_id=1, source_target_pairs={{0,8},{8,16},{16,24},{24,32},{32,40},{40,48},{48,56},{56,64},{64,7... | collective-permute-start | bytes 2359304 | tf_op jit(solution)/shard_map/ppermute | solution.py:15
  67.4 17.3 %collective-permute-start.3 = (bf16[6,8,8,8,128]{4,3,2,1,0:T(8,128)(2,1)}, bf16[6,8,8,8,128]{4,3,2,1,0:T(8,128)(2,1)S(1)}, u32[]{:S(2)}, u32[]{:S(2)}) collective-permute-start(bf16[6,8,8,8,128]{4,3,2,1,0:T(8,128)(2,1)} %gather_fusion.3), channel_id=1, source_target_pairs={{8,0},{16,8},{24,16},{32,24},{40,32},{48,40},{56,48},{64,56},{72,6... | collective-permute-start | bytes 2359304 | tf_op jit(solution)/shard_map/ppermute | solution.py:15
  73.9 22.0 %collective-permute-start.10 = (bf16[6,8,8,8,128]{4,3,2,1,0:T(8,128)(2,1)}, bf16[6,8,8,8,128]{4,3,2,1,0:T(8,128)(2,1)S(1)}, u32[]{:S(2)}, u32[]{:S(2)}) collective-permute-start(bf16[6,8,8,8,128]{4,3,2,1,0:T(8,128)(2,1)} %gather_fusion.64), channel_id=1, source_target_pairs={{0,8},{8,16},{16,24},{24,32},{32,40},{40,48},{48,56},{56,64},{64,7... | collective-permute-start | bytes 2359304 | tf_op jit(solution)/shard_map/ppermute | solution.py:15
  77.6 22.8 %collective-permute-start.11 = (bf16[6,8,8,8,128]{4,3,2,1,0:T(8,128)(2,1)}, bf16[6,8,8,8,128]{4,3,2,1,0:T(8,128)(2,1)S(1)}, u32[]{:S(2)}, u32[]{:S(2)}) collective-permute-start(bf16[6,8,8,8,128]{4,3,2,1,0:T(8,128)(2,1)} %gather_fusion.65), channel_id=1, source_target_pairs={{8,0},{16,8},{24,16},{32,24},{40,32},{48,40},{56,48},{64,56},{72,6... | collective-permute-start | bytes 2359304 | tf_op jit(solution)/shard_map/ppermute | solution.py:15
  147.8 84.0 %copy-start.8 = (bf16[19,8,8,1,128]{4,3,2,1,0:T(2,128)(2,1)S(1)}, bf16[19,8,8,1,128]{4,3,2,1,0:T(2,128)(2,1)}, u32[]{:S(2)}) copy-start(bf16[19,8,8,1,128]{4,3,2,1,0:T(2,128)(2,1)} %get-tuple-element.58) | copy-start | bytes 933892
  290.1 56.3 %copy-start.18 = (bf16[1,8,8,8,128]{4,3,2,1,0:T(8,128)(2,1)S(1)}, bf16[1,8,8,8,128]{4,3,2,1,0:T(8,128)(2,1)}, u32[]{:S(2)}) copy-start(bf16[1,8,8,8,128]{4,3,2,1,0:T(8,128)(2,1)} %copy-done.17) | copy-start | bytes 393220
  293.1 30.5 %collective-permute-start.12 = (bf16[2,8,8,8,128]{4,3,2,1,0:T(8,128)(2,1)}, bf16[2,8,8,8,128]{4,3,2,1,0:T(8,128)(2,1)S(1)}, u32[]{:S(2)}, u32[]{:S(2)}) collective-permute-start(bf16[2,8,8,8,128]{4,3,2,1,0:T(8,128)(2,1)} %gather_fusion.93), channel_id=1, source_target_pairs={{0,1},{1,2},{2,3},{3,4},{4,5},{5,6},{6,7},{8,9},{9,10},{10,11},{11... | collective-permute-start | bytes 786440 | tf_op jit(solution)/shard_map/ppermute | solution.py:15
  310.7 24.3 %collective-permute-start.13 = (bf16[2,8,8,8,128]{4,3,2,1,0:T(8,128)(2,1)}, bf16[2,8,8,8,128]{4,3,2,1,0:T(8,128)(2,1)S(1)}, u32[]{:S(2)}, u32[]{:S(2)}) collective-permute-start(bf16[2,8,8,8,128]{4,3,2,1,0:T(8,128)(2,1)} %gather_fusion.94), channel_id=1, source_target_pairs={{1,0},{2,1},{3,2},{4,3},{5,4},{6,5},{7,6},{9,8},{10,9},{11,10},{12... | collective-permute-start | bytes 786440 | tf_op jit(solution)/shard_map/ppermute | solution.py:15
  312.0 23.0 %collective-permute-start.4 = (bf16[2,8,8,8,128]{4,3,2,1,0:T(8,128)(2,1)}, bf16[2,8,8,8,128]{4,3,2,1,0:T(8,128)(2,1)S(1)}, u32[]{:S(2)}, u32[]{:S(2)}) collective-permute-start(bf16[2,8,8,8,128]{4,3,2,1,0:T(8,128)(2,1)} %gather_fusion.31), channel_id=1, source_target_pairs={{0,1},{1,2},{2,3},{3,4},{4,5},{5,6},{6,7},{8,9},{9,10},{10,11},{11... | collective-permute-start | bytes 786440 | tf_op jit(solution)/shard_map/ppermute | solution.py:15
  319.9 26.4 %collective-permute-start.5 = (bf16[2,8,8,8,128]{4,3,2,1,0:T(8,128)(2,1)}, bf16[2,8,8,8,128]{4,3,2,1,0:T(8,128)(2,1)}, u32[]{:S(2)}, u32[]{:S(2)}) collective-permute-start(bf16[2,8,8,8,128]{4,3,2,1,0:T(8,128)(2,1)} %gather_fusion.32), channel_id=1, source_target_pairs={{1,0},{2,1},{3,2},{4,3},{5,4},{6,5},{7,6},{9,8},{10,9},{11,10},{12... | collective-permute-start | bytes 786440 | tf_op jit(solution)/shard_map/ppermute | solution.py:15
  349.2 27.2 %collective-permute-start.6 = (bf16[6,8,8,8,128]{4,3,2,1,0:T(8,128)(2,1)}, bf16[6,8,8,8,128]{4,3,2,1,0:T(8,128)(2,1)}, u32[]{:S(2)}, u32[]{:S(2)}) collective-permute-start(bf16[6,8,8,8,128]{4,3,2,1,0:T(8,128)(2,1)} %gather_fusion.33), channel_id=1, source_target_pairs={{0,8},{8,16},{16,24},{24,32},{32,40},{40,48},{48,56},{56,64},{64,7... | collective-permute-start | bytes 2359304 | tf_op jit(solution)/shard_map/ppermute | solution.py:15
  359.9 18.5 %collective-permute-start.7 = (bf16[6,8,8,8,128]{4,3,2,1,0:T(8,128)(2,1)}, bf16[6,8,8,8,128]{4,3,2,1,0:T(8,128)(2,1)}, u32[]{:S(2)}, u32[]{:S(2)}) collective-permute-start(bf16[6,8,8,8,128]{4,3,2,1,0:T(8,128)(2,1)} %gather_fusion.34), channel_id=1, source_target_pairs={{8,0},{16,8},{24,16},{32,24},{40,32},{48,40},{56,48},{64,56},{72,6... | collective-permute-start | bytes 2359304 | tf_op jit(solution)/shard_map/ppermute | solution.py:15
  367.3 23.6 %collective-permute-start.14 = (bf16[6,8,8,8,128]{4,3,2,1,0:T(8,128)(2,1)}, bf16[6,8,8,8,128]{4,3,2,1,0:T(8,128)(2,1)S(1)}, u32[]{:S(2)}, u32[]{:S(2)}) collective-permute-start(bf16[6,8,8,8,128]{4,3,2,1,0:T(8,128)(2,1)} %gather_fusion.95), channel_id=1, source_target_pairs={{0,8},{8,16},{16,24},{24,32},{32,40},{40,48},{48,56},{56,64},{64,7... | collective-permute-start | bytes 2359304 | tf_op jit(solution)/shard_map/ppermute | solution.py:15
  370.4 29.9 %collective-permute-start.15 = (bf16[6,8,8,8,128]{4,3,2,1,0:T(8,128)(2,1)}, bf16[6,8,8,8,128]{4,3,2,1,0:T(8,128)(2,1)}, u32[]{:S(2)}, u32[]{:S(2)}) collective-permute-start(bf16[6,8,8,8,128]{4,3,2,1,0:T(8,128)(2,1)} %gather_fusion.96), channel_id=1, source_target_pairs={{8,0},{16,8},{24,16},{32,24},{40,32},{48,40},{56,48},{64,56},{72,6... | collective-permute-start | bytes 2359304 | tf_op jit(solution)/shard_map/ppermute | solution.py:15
  409.9 39.6 %copy-start.10 = (bf16[19,8,8,1,128]{4,3,2,1,0:T(2,128)(2,1)S(1)}, bf16[19,8,8,1,128]{4,3,2,1,0:T(2,128)(2,1)}, u32[]{:S(2)}) copy-start(bf16[19,8,8,1,128]{4,3,2,1,0:T(2,128)(2,1)} %get-tuple-element.85) | copy-start | bytes 933892
  450.3 58.8 %copy-start.13 = (bf16[2,8,8,1,128]{4,3,2,1,0:T(2,128)(2,1)}, bf16[2,8,8,1,128]{4,3,2,1,0:T(2,128)(2,1)S(1)}, u32[]{:S(2)}) copy-start(bf16[2,8,8,1,128]{4,3,2,1,0:T(2,128)(2,1)S(1)} %copy.209) | copy-start | bytes 98308
  450.5 65.7 %copy-start.9 = (bf16[19,8,8,1,128]{4,3,2,1,0:T(2,128)(2,1)S(1)}, bf16[19,8,8,1,128]{4,3,2,1,0:T(2,128)(2,1)}, u32[]{:S(2)}) copy-start(bf16[19,8,8,1,128]{4,3,2,1,0:T(2,128)(2,1)} %get-tuple-element.33) | copy-start | bytes 933892
  (87 other events, 748.8 us)
Sparse Core Ops, SparseCore 0:
  559.4 277.7 all-reduce.6
where the time goes:
time: 861 us; the launch traced here: 849 us
  local copies, waits for them, and re-layouts  408 us (47%)
  waiting for transfers between devices  295 us (34%)
  starting transfers between devices  70.6 us (8%)
  other arithmetic  35.3 us (4%)
  matrix products  22.9 us (3%)
  between operations  16.4 us (2%)
    psum x1, waiting for transfers between devices, on_device(): sum_one, sum_two = lax.psum((sum_one, sum_two), ('gx', 'gy'))  264 us
    gather x180, local copies, waits for them, and re-layouts, gather_block(): layers_z.append(portion[neighbours[:, 9 * off_x + 3 * off_y + off_z]])  186 us
    unnamed x387, local copies, waits for them, and re-layouts  122 us
    ppermute x16, starting transfers between devices, shifted(): return lax.ppermute(block, axis, route)  70.6 us
    slice x24, local copies, waits for them, and re-layouts, cut_layer(): return lax.slice_in_dim(portion, extent - 1, extent, axis=along_axis)  43.2 us
    ppermute x16, waiting for transfers between devices, shifted(): return lax.ppermute(block, axis, route)  31.1 us
    gather x16, local copies, waits for them, and re-layouts, pick_rows(): return padded_rows[clipped]  24.3 us
    another operation x8, local copies, waits for them, and re-layouts, to_columns(): stacked = jnp.stack(tap_list, axis=4)  20.3 us
  transfers between devices with their start and end apart: 17, of which 4 were waited for; matrix products, arithmetic and copies ran while one was open for 12% of the time, Pallas kernels for 0%

commit v1 on v0

v1 whole, which is shorter than its diff:
```python
import functools
import math

import jax
import jax.numpy as jnp
from jax import lax
from jax.experimental import pallas as pl
from jax.experimental.pallas import tpu as pltpu
from jax.sharding import PartitionSpec as P

EDGE = 8
KVOL = 27
CH = 128
PLANE = EDGE * EDGE
NONE = 18
BF = jnp.bfloat16
F32 = jnp.float32
MESH = pl.DeviceIdType.MESH
SLICE = (4, 4, 2, 4, 2)


def chunk_rows(slice_dims):
    nx, ny, zhi, zlo, _ = slice_dims
    rows = KVOL * CH
    plane = -(-rows // (nx * ny * 16)) * 16
    line = -(-plane // (zhi * zlo * 16)) * 16
    return plane, line


def with_z(line, below, above):
    n = line.shape[0]
    flat = lambda t: t.reshape(n * 2, EDGE, CH)
    line, below, above = flat(line), flat(below), flat(above)
    level = lax.broadcasted_iota(jnp.int32, line.shape, 1)
    down = pltpu.roll(jnp.where(level == EDGE - 1, below, line), 1, 1)
    up = pltpu.roll(jnp.where(level == 0, above, line), EDGE - 1, 1)
    return [t.reshape(n, 2 * EDGE, CH).astype(BF) for t in (down, line, up)]


def put(z_ref, f, px, qy, line, below, above):
    for e, rows in enumerate(with_z(line, below, above)):
        z_ref[f, px, qy, :, e * CH : (e + 1) * CH] = rows


def kernel(dims, scale, *refs):
    (
        feat, occ, w1_hbm, bias, w2_hbm, cot, nbr, sx, sy,
        out_ref, gf_ref, gw_ref,
        w1, w2, mask, fa, fb, za, zb, at,
        xfa, yfa, eda, edla, xsa, ysa, esa,
        xfb, yfb, edb, edlb, xsb, ysb, esb,
        gwo, gwm, crecv, rs1, zs1, rz, ag1,
        w_sem, halo_s, halo_r, core_s, core_r, p_s, p_r, l_s, l_r, m_s, m_r, g_s, g_r, f_s, f_r,
    ) = refs
    nx, ny, nzhi, nzlo, _ = dims
    nz = nzhi * nzlo
    plane_rows, line_rows = chunk_rows(dims)
    ngx, ngy = nzlo * ny * 2, nx * nzhi
    gx, gy = lax.axis_index("gx"), lax.axis_index("gy")
    core = lax.rem(gx, 2)
    y = lax.rem(gx // 2, ny)
    z = lax.rem(gy, nzhi) * nzlo + gx // (2 * ny)
    x = gy // nzhi

    def device(px, py, pz, c):
        return (lax.rem(pz, nzlo) * (2 * ny) + py * 2 + c, px * nzhi + pz // nzlo)

    next_x = (lax.rem(gx + 1, ngx), gy)
    prev_x = (lax.rem(gx + ngx - 1, ngx), gy)
    next_y = (gx, lax.rem(gy + 1, ngy))
    prev_y = (gx, lax.rem(gy + ngy - 1, ngy))
    partner = device(x, y, z, 1 - core)
    offsets = [(i, k) for i in range(nx) for k in range(ny) if (i, k) != (0, 0)]
    plane_peer = {o: (lax.rem(x + o[0], nx), lax.rem(y + o[1], ny)) for o in offsets}
    line_peer = {d: lax.rem(z + d, nz) for d in range(1, nz)}

    barrier = pltpu.get_barrier_semaphore()
    greet = [next_x, prev_x, next_y, prev_y]
    greet += [device(*plane_peer[o], z, core) for o in offsets]
    greet += [device(x, y, line_peer[d], core) for d in line_peer]
    for who in greet:
        pl.semaphore_signal(barrier, inc=1, device_id=who, device_id_type=MESH)
    load_w1 = pltpu.make_async_copy(w1_hbm, w1, w_sem.at[0])
    load_w2 = pltpu.make_async_copy(w2_hbm, w2, w_sem.at[1])
    load_w1.start()
    load_w2.start()

    for t in range(4):
        halves = []
        for b in range(2):
            live = (nbr[b, 13] != NONE).astype(F32)
            row = occ[b : b + 1, t * CH : (t + 1) * CH].astype(F32) * live
            halves.append(jnp.broadcast_to(row, (CH, CH)).T.reshape(16, EDGE, CH))
        mask[t * 16 : (t + 1) * 16] = jnp.stack(halves, 1).reshape(16, 16, CH)

    def fields(p, carry):
        mk = mask[pl.ds(p * EDGE, EDGE)]
        rows = pl.ds(pl.multiple_of(p * PLANE, PLANE), PLANE)
        for f, source in enumerate((feat, cot)):
            both = jnp.stack(
                [source[b, rows].astype(F32).reshape(EDGE, EDGE, CH) for b in range(2)], 1
            )
            fa[f, pl.ds(p * EDGE, EDGE)] = (both.reshape(EDGE, 16, CH) * mk).astype(BF)
        return carry

    lax.fori_loop(0, EDGE, fields, 0)

    def remote(src, dst, send, recv, who):
        return pltpu.make_async_remote_copy(
            src_ref=src, dst_ref=dst, send_sem=send, recv_sem=recv, device_id=who, device_id_type=MESH
        )

    def own_faces(field, xf, yf, ed, edl, xs, ys):
        for side in range(2):
            xf[side, NONE] = jnp.zeros(xf.shape[2:], BF)
            yf[side, 6] = jnp.zeros(yf.shape[2:], BF)
            ed[side, NONE] = jnp.zeros(ed.shape[2:], BF)
            edl[side, 6] = jnp.zeros(edl.shape[2:], BF)
            edge = (1 - side) * (EDGE - 1)
            for f in range(2):
                faces = field[f, edge * EDGE : (edge + 1) * EDGE].astype(F32).reshape(EDGE, 2, EDGE, CH)
                walls = jnp.stack([field[f, p * EDGE + edge].astype(F32) for p in range(EDGE)], 0)
                walls = walls.reshape(EDGE, 2, EDGE, CH)
                face = [faces[:, b].reshape(PLANE, CH) for b in range(2)]
                wall = [walls[:, b].reshape(PLANE, CH) for b in range(2)]
                for b in range(2):
                    xf[side, b, f] = face[b].astype(BF)
                    yf[side, b, f] = wall[b].astype(BF)
                    lines = jnp.concatenate([face[b][:EDGE], face[b][PLANE - EDGE :]], 0)
                    edl[side, b, f] = lines.astype(BF)
                for r in range(2):
                    for listed, picks, sent in ((sx, face, xs), (sy, wall, ys)):
                        slot = listed[side, r]
                        low = jnp.where(slot == 0, picks[0], 0.0)
                        sent[side, r, f] = jnp.where(slot == 1, picks[1], low).astype(BF)

    def halo_copies(ph, xf, yf, ed, xs, ys, es):
        def go(n, src, dst, who):
            return remote(src, dst, halo_s.at[ph, n], halo_r.at[ph, n], who)

        walls = [go(0, ys.at[0], yf.at[0, 2:4], next_y), go(1, ys.at[1], yf.at[1, 4:6], prev_y)]
        faces = [go(2, xs.at[0], xf.at[0, 6:8], next_x), go(3, xs.at[1], xf.at[1, 12:14], prev_x)]
        lines = [go(4, es.at[0], ed.at[0, 6:12], next_x), go(5, es.at[1], ed.at[1, 12:18], prev_x)]
        return walls, faces, lines

    def edge_lines(yf, ed, edl, es):
        blank = jnp.zeros((EDGE, CH), F32)
        for f in range(2):
            for r in range(2, 6):
                got = yf[(r - 2) // 2, r, f].astype(F32)
                for side, line in ((0, got[PLANE - EDGE :]), (1, got[:EDGE])):
                    pair = [blank, line] if r < 4 else [line, blank]
                    edl[side, r, f] = jnp.concatenate(pair, 0).astype(BF)
        for side in range(2):
            for r in range(6):
                es[side, r] = edl[side, jnp.minimum(sx[side, r], 6)]
                ed[side, r] = edl[side, r]

    def inner(field, z_ref):
        linked = [[(nbr[b, 12 + 2 * d] != NONE).astype(F32) for b in range(2)] for d in range(2)]

        def plane(p, carry):
            for f in range(2):
                line = field[f, pl.ds(p * EDGE, EDGE)].astype(F32).reshape(EDGE, 2, EDGE, CH)
                near = [
                    jnp.stack([line[:, 1] * linked[d][0], line[:, 0] * linked[d][1]], 1) for d in range(2)
                ]
                put(z_ref, f, p + 1, slice(1, EDGE + 1), line, *near)
            return carry

        lax.fori_loop(0, EDGE, plane, 0)

    def shell(z_ref, xf, yf, ed):
        def three(first, load):
            pick = lambda k: jnp.stack([load(nbr[b, k]).astype(F32) for b in range(2)], 1)
            return pick(first + 1), pick(first), pick(first + 2)

        for f in range(2):
            for side in range(2):
                far = slice((EDGE + 1) * side, (EDGE + 1) * side + 1)
                core_part = slice(1, EDGE + 1)
                faces = three(18 * side + 3, lambda r: xf[side, r, f].reshape(EDGE, EDGE, CH))
                for e, rows in enumerate(with_z(*faces)):
                    z_ref[f, (EDGE + 1) * side, core_part, :, e * CH : (e + 1) * CH] = rows
                walls = three(
                    9 + 6 * side, lambda r: yf[side, jnp.minimum(r, 6), f].reshape(EDGE, EDGE, CH)
                )
                for e, rows in enumerate(with_z(*walls)):
                    z_ref[f, core_part, (EDGE + 1) * side, :, e * CH : (e + 1) * CH] = rows
                for up in range(2):
                    low = (1 - up) * EDGE
                    lines = three(
                        18 * side + 6 * up,
                        lambda r: ed[side, r, f].astype(F32)[low : low + EDGE].reshape(1, EDGE, CH),
                    )
                    for e, rows in enumerate(with_z(*lines)):
                        z_ref[f, (EDGE + 1) * side, (EDGE + 1) * up, :, e * CH : (e + 1) * CH] = rows[0]

    half = 2
    taps = [(a, c) for a in range(3) for c in range(3)]

    def columns(z_ref, f, m):
        parts = [
            z_ref[f, pl.ds(m * half + a, half), c : c + EDGE].reshape(half * EDGE * 16, 3 * CH)
            for a, c in taps
        ]
        return jnp.concatenate(parts, 1)

    def conv(z_ref, f, m, w):
        return jnp.dot(columns(z_ref, f, m), w[...], preferred_element_type=F32)

    def conv_t(z_ref, f, m, w):
        turned = jnp.concatenate([w[(KVOL - 1 - k) * CH : (KVOL - k) * CH] for k in range(KVOL)], 1)
        return lax.dot_general(
            columns(z_ref, f, m), turned, (((1,), (1,)), ((), ())), preferred_element_type=F32
        )

    own_faces(fa, xfa, yfa, eda, edla, xsa, ysa)
    walls_a, faces_a, lines_a = halo_copies(0, xfa, yfa, eda, xsa, ysa, esa)
    pl.semaphore_wait(barrier, len(greet))
    for copy in walls_a + faces_a:
        copy.start()
    inner(fa, za)
    for copy in walls_a:
        copy.wait()
    edge_lines(yfa, eda, edla, esa)
    for copy in lines_a:
        copy.start()
    for copy in faces_a + lines_a:
        copy.wait()
    shell(za, xfa, yfa, eda)
    load_w1.wait()
    load_w2.wait()

    tiles = half * EDGE
    steps = EDGE // half

    def first_layer(m, carry):
        part = pl.ds(m * tiles, tiles)
        mk = mask[part].reshape(tiles * 16, CH)
        preact = conv(za, 0, m, w1) + bias[...]
        back = conv_t(za, 1, m, w2)
        hidden = (jnp.maximum(preact, 0.0) * mk).astype(BF)
        grad = jnp.where(preact > 0, back * mk, 0.0).astype(BF)
        fb[0, part] = hidden.reshape(tiles, 16, CH)
        fb[1, part] = grad.reshape(tiles, 16, CH)
        at[0, m] = grad.T
        at[1, m] = hidden.T
        return carry

    lax.fori_loop(0, steps, first_layer, 0)

    own_faces(fb, xfb, yfb, edb, edlb, xsb, ysb)
    walls_b, faces_b, lines_b = halo_copies(1, xfb, yfb, edb, xsb, ysb, esb)
    for copy in walls_b + faces_b:
        copy.start()

    third = 9 * CH

    def weight_grad(which, a, dst, add=None):
        left = jnp.concatenate([at[which, i] for i in range(steps)], 1)
        first = which == 0
        pa = jnp.where(first, a, 2 - a)
        for c in range(3):
            pc = jnp.where(first, c, 2 - c)
            right = za[which, pl.ds(pa, EDGE), pl.ds(pc, EDGE)].reshape(EDGE * EDGE * 16, 3 * CH)
            prod = jnp.dot(left, right, preferred_element_type=F32)
            for e in range(3):
                plain = prod[:, (2 - e) * CH : (3 - e) * CH]
                turned = prod[:, e * CH : (e + 1) * CH].T
                block = jnp.where(first, turned, plain)
                row = (9 * a + 3 * c + e) * CH
                if add is not None:
                    block = block + add[row : row + CH].astype(F32)
                dst[row : row + CH] = block.astype(BF)

    core_copies = [
        remote(
            gwo.at[a * third : (a + 1) * third],
            crecv.at[a * third : (a + 1) * third],
            core_s.at[a],
            core_r.at[a],
            partner,
        )
        for a in range(3)
    ]
    for a in range(3):
        weight_grad(1 - core, a, gwo)
        core_copies[a].start()
    for copy in walls_b:
        copy.wait()
    edge_lines(yfb, edb, edlb, esb)
    for copy in lines_b:
        copy.start()
    for a in range(3):
        core_copies[a].wait()
        weight_grad(core, a, gwm, crecv)
    if gwm.shape[0] > KVOL * CH:
        gwm[KVOL * CH :] = jnp.zeros((gwm.shape[0] - KVOL * CH, CH), BF)

    def rows_of(index, n):
        return pl.ds(pl.multiple_of(index * n, 16), n)

    me = x * ny + y
    plane_copies = {}
    for o in offsets:
        px, py = plane_peer[o]
        n = o[0] * ny + o[1]
        plane_copies[o] = remote(
            gwm.at[rows_of(px * ny + py, plane_rows)], rs1.at[n], p_s.at[n], p_r.at[n], device(px, py, z, core)
        )
        plane_copies[o].start()

    for copy in faces_b + lines_b:
        copy.wait()
    inner(fb, zb)
    shell(zb, xfb, yfb, edb)

    def second_layer(m, carry):
        part = pl.ds(m * tiles, tiles)
        mk = mask[part].reshape(tiles * 16, CH)
        masked = fa[0, part].astype(F32).reshape(tiles * 16, CH)
        given = fa[1, part].astype(F32).reshape(tiles * 16, CH)
        result = conv(zb, 0, m, w2) * mk + masked
        grad = conv_t(zb, 1, m, w1) * mk + given
        rows = pl.ds(pl.multiple_of(m * tiles * EDGE, tiles * EDGE), tiles * EDGE)
        for value, dst in ((result, out_ref), (grad, gf_ref)):
            bricks = value.reshape(tiles, 2, EDGE, CH)
            for b in range(2):
                dst[b, rows] = bricks[:, b].reshape(tiles * EDGE, CH).astype(BF)
        return carry

    lax.fori_loop(0, steps, second_layer, 0)

    for o in offsets:
        plane_copies[o].wait()

    def plane_sum(t, carry):
        start = pl.multiple_of(t * 16, 16)
        total = gwm[pl.ds(pl.multiple_of(me * plane_rows + start, 16), 16)].astype(F32)
        for i, k in offsets:
            total = total + rs1[i * ny + k, pl.ds(start, 16)].astype(F32)
        zs1[pl.ds(start, 16)] = total.astype(BF)
        return carry

    lax.fori_loop(0, plane_rows // 16, plane_sum, 0)
    if zs1.shape[0] > plane_rows:
        zs1[plane_rows:] = jnp.zeros((zs1.shape[0] - plane_rows, CH), BF)

    line_copies = [
        remote(zs1.at[rows_of(pz, line_rows)], rz.at[d], l_s.at[d], l_r.at[d], device(x, y, pz, core))
        for d, pz in line_peer.items()
    ]
    for copy in line_copies:
        copy.start()
    for copy in line_copies:
        copy.wait()
    mine = rows_of(z, line_rows)
    total = zs1[mine].astype(F32)
    for d in line_peer:
        total = total + rz[d].astype(F32)
    ag1[mine] = (total * scale).astype(BF)

    back_copies = [
        remote(ag1.at[mine], ag1.at[mine], m_s.at[d], m_r.at[d], device(x, y, pz, core))
        for d, pz in line_peer.items()
    ]
    for copy in back_copies:
        copy.start()
    for copy in back_copies:
        copy.wait()
    home = rows_of(me, plane_rows)
    gather = {}
    for i, k in offsets:
        n = i * ny + k
        gather[i, k] = remote(
            ag1.at[:plane_rows], gw_ref.at[core, home], g_s.at[n], g_r.at[n], device(*plane_peer[i, k], z, core)
        )
        gather[i, k].start()
    gw_ref[core, home] = ag1[:plane_rows]
    forward = [remote(gw_ref.at[core, home], gw_ref.at[core, home], f_s.at[0], f_r.at[0], partner)]
    forward[0].start()
    for i, k in offsets:
        n = i * ny + k
        gather[i, k].wait()
        held = rows_of(lax.rem(x + nx - i, nx) * ny + lax.rem(y + ny - k, ny), plane_rows)
        forward.append(remote(gw_ref.at[core, held], gw_ref.at[core, held], f_s.at[n], f_r.at[n], partner))
        forward[-1].start()
    for copy in forward:
        copy.wait()


def on_device(dims, features, occupied, weight_one, bias_one, weight_two, cotangent, neighbours, send_x, send_y):
    nx, ny, nzhi, nzlo, _ = dims
    nz, nxy = nzhi * nzlo, nx * ny
    plane_rows, line_rows = chunk_rows(dims)
    devices = 2 * nxy * nz
    slots, voxels, _ = features.shape
    scale = 1.0 / math.sqrt(slots * voxels * devices)
    vmem = pl.BlockSpec(memory_space=pltpu.VMEM)
    smem = pl.BlockSpec(memory_space=pltpu.SMEM)
    hbm = pl.BlockSpec(memory_space=pl.ANY)
    rows = KVOL * CH

    def halo():
        return [
            pltpu.VMEM((2, NONE + 1, 2, PLANE, CH), BF),
            pltpu.VMEM((2, 7, 2, PLANE, CH), BF),
            pltpu.VMEM((2, NONE + 1, 2, 16, CH), BF),
            pltpu.VMEM((2, 7, 2, 16, CH), BF),
            pltpu.VMEM((2, 2, 2, PLANE, CH), BF),
            pltpu.VMEM((2, 2, 2, PLANE, CH), BF),
            pltpu.VMEM((2, 6, 2, 16, CH), BF),
        ]

    field = pltpu.VMEM((2, PLANE, 16, CH), BF)
    padded = pltpu.VMEM((2, EDGE + 2, EDGE + 2, 16, 3 * CH), BF)
    sem = lambda *shape: pltpu.SemaphoreType.DMA(shape)
    out, grad_features, grads = pl.pallas_call(
        functools.partial(kernel, dims, scale),
        out_shape=(
            jax.ShapeDtypeStruct(features.shape, BF),
            jax.ShapeDtypeStruct(features.shape, BF),
            jax.ShapeDtypeStruct((2, nxy * plane_rows, CH), BF),
        ),
        in_specs=[vmem, vmem, hbm, vmem, hbm, vmem, smem, smem, smem],
        out_specs=(vmem, vmem, vmem),
        scratch_shapes=[
            pltpu.VMEM((rows, CH), BF),
            pltpu.VMEM((rows, CH), BF),
            pltpu.VMEM((PLANE, 16, CH), F32),
            field,
            field,
            padded,
            padded,
            pltpu.VMEM((2, 4, CH, 256), BF),
            *halo(),
            *halo(),
            pltpu.VMEM((rows, CH), BF),
            pltpu.VMEM((nxy * plane_rows, CH), BF),
            pltpu.VMEM((rows, CH), BF),
            pltpu.VMEM((nxy, plane_rows, CH), BF),
            pltpu.VMEM((nz * line_rows, CH), BF),
            pltpu.VMEM((nz, line_rows, CH), BF),
            pltpu.VMEM((nz * line_rows, CH), BF),
            sem(2),
            sem(2, 6), sem(2, 6),
            sem(3), sem(3),
            sem(nxy), sem(nxy),
            sem(nz), sem(nz),
            sem(nz), sem(nz),
            sem(nxy), sem(nxy),
            sem(nxy), sem(nxy),
        ],
        compiler_params=pltpu.CompilerParams(
            collective_id=0, has_side_effects=True, vmem_limit_bytes=56 * 2**20
        ),
    )(
        features,
        occupied,
        weight_one.reshape(rows, CH),
        bias_one.reshape(1, CH),
        weight_two.reshape(rows, CH),
        cotangent,
        neighbours,
        send_x.reshape(2, -1),
        send_y.reshape(2, -1),
    )
    one, two = (grads[j, :rows].astype(F32).reshape(KVOL, CH, CH) for j in range(2))
    return (out, grad_features, one, two)


def solution(mesh, dims=SLICE):
    in_specs = (
        P(("gx", "gy"), None, None),
        P(("gx", "gy"), None),
        P(),
        P(),
        P(),
        P(("gx", "gy"), None, None),
        P(("gx", "gy"), None),
        P(("gx", "gy"), None, None),
        P(("gx", "gy"), None, None),
    )
    out_specs = (P(("gx", "gy"), None, None), P(("gx", "gy"), None, None), P(), P())
    return jax.shard_map(
        functools.partial(on_device, dims), mesh=mesh, in_specs=in_specs, out_specs=out_specs, check_vma=False
    )
```

time: 861 us -> 89.5 us (0.10); the launches traced: 849 us -> 89.4 us
  local copies, waits for them, and re-layouts: 408 us -> 2.96 us
  waiting for transfers between devices: 295 us -> 0 us
  Pallas kernels: 0 us -> 82.9 us
  starting transfers between devices: 70.6 us -> 0 us
  other arithmetic: 35.3 us -> 2.81 us
  matrix products: 22.9 us -> 0 us
  between operations: 16.4 us -> 0.65 us
    psum x1 -> x0, waiting for transfers between devices: 264 us -> none  [on_device(): sum_one, sum_two = lax.psum((sum_one, sum_two), ('gx', 'gy'))]
    gather x196 -> x0, local copies, waits for them, and re-layouts: 210 us -> none  [the longest x180 186 us: gather_block(): layers_z.append(portion[neighbours[:, 9 * off_x + 3 * off_y + off_z]])]
    unnamed x387 -> x6, local copies, waits for them, and re-layouts: 122 us -> 1.41 us
    pallas_call x0 -> x1, Pallas kernels: none -> 82.9 us  [on_device(): pl.pallas_call(functools.partial(kernel, dims, scale), out_shape=(jax.Sha...]
    ppermute x16 -> x0, starting transfers between devices: 70.6 us -> none  [shifted(): return lax.ppermute(block, axis, route)]
    slice x30 -> x1, local copies, waits for them, and re-layouts: 51.2 us -> 1.55 us  [on_device(): grads[j, :rows].astype(F32).reshape(KVOL, CH, CH)]
    ppermute x16 -> x0, waiting for transfers between devices: 31.1 us -> none  [shifted(): return lax.ppermute(block, axis, route)]
    dot_general x6 -> x0, matrix products: 22.9 us -> none  [the longest x1 6.26 us: on_device(): lax.dot_general(cols_input, grad_hidden.reshape(slots * voxels, channels)...]
  transfers between devices with their start and end apart: 17 -> 0, of which waited for: 4 -> 0; matrix products, arithmetic and copies ran while one was open for 12% -> 0% of each run, Pallas kernels for 0% -> 0%
where the time goes in v1:
time: 89.5 us; the launch traced here: 89.4 us
  Pallas kernels  82.9 us (93%)
  local copies, waits for them, and re-layouts  2.96 us (3%)
  other arithmetic  2.81 us (3%)
    pallas_call x1, Pallas kernels, on_device(): pl.pallas_call(functools.partial(kernel, dims, scale), out_shape=(jax.Sha...  82.9 us
    convert_element_type x2, other arithmetic, on_device(): grads[j, :rows].astype(F32).reshape(KVOL, CH, CH)  2.81 us

profile of v1, /device:TPU:1, one launch (start us, length us, event | category | flops | bytes accessed | tf_op | source)
XLA Modules:
  0.0 89.4 jit_solution(7427650548003310667)
XLA Ops:
  0.6 82.9 %shard_map.120 = (bf16[2,512,128]{2,1,0:T(8,128)(2,1)}, bf16[2,512,128]{2,1,0:T(8,128)(2,1)}, bf16[2,3584,128]{2,1,0:T(8,128)(2,1)}) custom-call(bf16[2,512,128]{2,1,0:T(8,128)(2,1)} %refs_0_.1, s32[2,512]{1,0:T(2,128)} %refs_1_.1, bf16[3456,128]{1,0:T(8,128)(2,1)} %bitcast.11, f32[1,128]{1,0:T(1,128)} %bitcast.15, bf16[3456,128]{1,0:T(8,128)(2,1)} %bitcast.12, ...), custom_call_target="tpu_custom_call" | custom-call | tf_op jit(solution)/shard_map/pallas_call | solution.py:419
  83.6 1.6 %fusion = (bf16[1,3456,128]{2,1,0:T(8,128)(2,1)S(1)}, bf16[1,3456,128]{2,1,0:T(8,128)(2,1)S(1)}) fusion(bf16[2,3584,128]{2,1,0:T(8,128)(2,1)} %get-tuple-element.9), kind=kLoop, calls=%fused_computation | loop fusion | bytes 3538944 | tf_op jit(solution)/shard_map/slice | solution.py:469
  85.1 1.4 %convert.2 = f32[27,128,128]{2,1,0:T(8,128)} convert(bf16[27,128,128]{2,1,0:T(8,128)(2,1)S(1)} %bitcast.10) | non-fusion elementwise | flops 442368 | bytes 2654208 | tf_op jit(solution)/shard_map/convert_element_type | solution.py:469
  86.5 0.0 copy-start.1
  86.5 0.0 copy-start
  86.5 1.4 %convert.3 = f32[27,128,128]{2,1,0:T(8,128)} convert(bf16[27,128,128]{2,1,0:T(8,128)(2,1)S(1)} %bitcast.9) | non-fusion elementwise | flops 442368 | bytes 2654208 | tf_op jit(solution)/shard_map/convert_element_type | solution.py:469
  87.9 0.0 copy-done.1
  88.0 0.7 copy.15
  88.7 0.0 copy-done
  88.7 0.7 copy.16
Async XLA Ops:
  86.5 1.4 %copy-start.1 = (bf16[2,512,128]{2,1,0:T(8,128)(2,1)S(1)}, bf16[2,512,128]{2,1,0:T(8,128)(2,1)}, u32[]{:S(2)}) copy-start(bf16[2,512,128]{2,1,0:T(8,128)(2,1)} %get-tuple-element.16) | copy-start | bytes 786436
  86.5 2.1 %copy-start = (bf16[2,512,128]{2,1,0:T(8,128)(2,1)S(1)}, bf16[2,512,128]{2,1,0:T(8,128)(2,1)}, u32[]{:S(2)}) copy-start(bf16[2,512,128]{2,1,0:T(8,128)(2,1)} %get-tuple-element.17) | copy-start | bytes 786436

commit v2 on v1

v2 whole, which is shorter than its diff:
```python
import functools
import math

import jax
import jax.numpy as jnp
from jax import lax
from jax.experimental import pallas as pl
from jax.experimental.pallas import tpu as pltpu
from jax.sharding import PartitionSpec as P

EDGE = 8
KVOL = 27
CH = 128
PLANE = EDGE * EDGE
NONE = 18
BF = jnp.bfloat16
F32 = jnp.float32
MESH = pl.DeviceIdType.MESH
SLICE = (4, 4, 2, 4, 2)


def with_z(line, below, above):
    n = line.shape[0]
    flat = lambda t: t.reshape(n * 2, EDGE, CH)
    line, below, above = flat(line), flat(below), flat(above)
    level = lax.broadcasted_iota(jnp.int32, line.shape, 1)
    down = pltpu.roll(jnp.where(level == EDGE - 1, below, line), 1, 1)
    up = pltpu.roll(jnp.where(level == 0, above, line), EDGE - 1, 1)
    return [t.reshape(n, 2 * EDGE, CH).astype(BF) for t in (down, line, up)]


class Part:
    def __init__(self, remote, local, result, base, rows, first, second, bufs, sems):
        self.remote, self.local, self.result = remote, local, result
        self.base, self.first, self.second = base, first, second
        self.got_one, self.partial, self.got_two, self.whole = bufs
        self.sems = sems
        self.one = rows // first.size
        self.two = self.got_two.shape[1]

    def rows(self, index, n, base=0):
        return pl.ds(pl.multiple_of(base + index * n, 16), n)

    def scatter_one(self):
        self.copies = []
        for n, who, index, _ in self.first.peers:
            src = self.local.at[self.rows(index, self.one, self.base)]
            self.copies.append(self.remote(src, self.got_one.at[n], self.sems[0].at[n], self.sems[1].at[n], who))
            self.copies[-1].start()

    def wait(self):
        for copy in self.copies:
            copy.wait()

    def scatter_two(self):
        self.wait()

        def tile(t, carry):
            start = pl.multiple_of(t * 16, 16)
            own = pl.ds(pl.multiple_of(self.base + self.first.me * self.one + start, 16), 16)
            total = self.local[own].astype(F32)
            for n, _, _, _ in self.first.peers:
                total = total + self.got_one[n, pl.ds(start, 16)].astype(F32)
            self.partial[pl.ds(start, 16)] = total.astype(BF)
            return carry

        lax.fori_loop(0, self.one // 16, tile, 0)
        spare = self.partial.shape[0] - self.one
        if spare:
            self.partial[self.one :] = jnp.zeros((spare, CH), BF)
        self.copies = []
        for n, who, index, _ in self.second.peers:
            src = self.partial.at[self.rows(index, self.two)]
            self.copies.append(self.remote(src, self.got_two.at[n], self.sems[2].at[n], self.sems[3].at[n], who))
            self.copies[-1].start()

    def gather_two(self, scale):
        self.wait()
        mine = self.rows(self.second.me, self.two)
        total = self.partial[mine].astype(F32)
        for n, _, _, _ in self.second.peers:
            total = total + self.got_two[n].astype(F32)
        self.whole[mine] = (total * scale).astype(BF)
        self.copies = []
        for n, who, _, _ in self.second.peers:
            block = self.whole.at[mine]
            self.copies.append(self.remote(block, block, self.sems[4].at[n], self.sems[5].at[n], who))
            self.copies[-1].start()

    def gather_one(self, core, partner):
        self.wait()
        home = self.rows(self.first.me, self.one, self.base)
        self.copies = []
        for n, who, _, _ in self.first.peers:
            src, dst = self.whole.at[: self.one], self.result.at[core, home]
            self.copies.append(self.remote(src, dst, self.sems[6].at[n], self.sems[7].at[n], who))
            self.copies[-1].start()
        self.result[core, home] = self.whole[: self.one]
        self.passed = []
        self.pass_on(core, partner, home, 0)

    def pass_on(self, core, partner, rows, n):
        block = self.result.at[core, rows]
        self.passed.append(self.remote(block, block, self.sems[8].at[n], self.sems[9].at[n], partner))
        self.passed[-1].start()

    def finish(self, core, partner, step):
        n, _, _, sender = self.first.peers[step]
        self.copies[step].wait()
        self.pass_on(core, partner, self.rows(sender, self.one, self.base), n)


class Group:
    def __init__(self, size, me, peers):
        self.size, self.me, self.peers = size, me, peers


class Halo:
    def __init__(self, refs):
        self.face, self.wall, self.edge, self.face_out, self.wall_out, self.diag_out, self.diag = refs


def kernel(dims, scale, *refs):
    (
        feat, occ, w1_hbm, bias, w2_hbm, cot, nbr, sx, sy,
        out_ref, gf_ref, gw_ref,
        w1, w2, mask, gate, fa0, fa1, fb0, fb1, za, zb, at, list_out, lists, gwo, gwm, crecv,
    ) = refs[:28]
    halos = [Halo(refs[28 + 7 * i : 35 + 7 * i]) for i in range(4)]
    bufs_q, bufs_p = refs[56:60], refs[60:64]
    w_sem, halo_s, halo_r, core_s, core_r = refs[64:69]
    sems_q, sems_p = refs[69:79], refs[79:89]
    nx, ny, nzhi, nzlo, _ = dims
    nz = nzhi * nzlo
    ngx, ngy = nzlo * ny * 2, nx * nzhi
    gx, gy = lax.axis_index("gx"), lax.axis_index("gy")
    core = lax.rem(gx, 2)
    y = lax.rem(gx // 2, ny)
    z = lax.rem(gy, nzhi) * nzlo + gx // (2 * ny)
    x = gy // nzhi

    def device(px, py, pz, c):
        return (lax.rem(pz, nzlo) * (2 * ny) + py * 2 + c, px * nzhi + pz // nzlo)

    near_x = [lax.rem(gx + 1, ngx), lax.rem(gx + ngx - 1, ngx)]
    near_y = [lax.rem(gy + 1, ngy), lax.rem(gy + ngy - 1, ngy)]
    partner = device(x, y, z, 1 - core)
    in_plane = []
    for i in range(nx):
        for k in range(ny):
            if i or k:
                px, py = lax.rem(x + i, nx), lax.rem(y + k, ny)
                back = lax.rem(x + nx - i, nx) * ny + lax.rem(y + ny - k, ny)
                in_plane.append((i * ny + k, device(px, py, z, core), px * ny + py, back))
    plane = Group(nx * ny, x * ny + y, in_plane)
    in_line = [
        (d, device(x, y, lax.rem(z + d, nz), core), lax.rem(z + d, nz), lax.rem(z + nz - d, nz))
        for d in range(1, nz)
    ]
    line = Group(nz, z, in_line)

    barrier = pltpu.get_barrier_semaphore()
    greet = [(px, gy) for px in near_x] + [(gx, py) for py in near_y]
    greet += [(px, py) for px in near_x for py in near_y]
    greet += [peer[1] for peer in in_plane + in_line]
    for who in greet:
        pl.semaphore_signal(barrier, inc=1, device_id=who, device_id_type=MESH)
    load_w1 = pltpu.make_async_copy(w1_hbm, w1, w_sem.at[0])
    load_w2 = pltpu.make_async_copy(w2_hbm, w2, w_sem.at[1])
    load_w1.start()
    load_w2.start()

    for t in range(4):
        halves = []
        for b in range(2):
            live = (nbr[b, 13] != NONE).astype(F32)
            row = occ[b : b + 1, t * CH : (t + 1) * CH].astype(F32) * live
            halves.append(jnp.broadcast_to(row, (CH, CH)).T.reshape(16, EDGE, CH))
        mask[t * 16 : (t + 1) * 16] = jnp.stack(halves, 1).reshape(16, 16, CH)

    def fields(p, carry):
        part = pl.ds(p * EDGE, EDGE)
        mk = mask[part]
        rows = pl.ds(pl.multiple_of(p * PLANE, PLANE), PLANE)
        for source, field in ((feat, fa0), (cot, fa1)):
            both = jnp.stack(
                [source[b, rows].astype(F32).reshape(EDGE, EDGE, CH) for b in range(2)], 1
            )
            field[part] = (both.reshape(EDGE, 16, CH) * mk).astype(BF)
        return carry

    lax.fori_loop(0, EDGE, fields, 0)

    def remote(src, dst, send, recv, who):
        return pltpu.make_async_remote_copy(
            src_ref=src, dst_ref=dst, send_sem=send, recv_sem=recv, device_id=who, device_id_type=MESH
        )

    def own_faces(field, halo):
        for side in range(2):
            halo.face[side, NONE] = jnp.zeros((PLANE, CH), BF)
            halo.wall[side, 6] = jnp.zeros((PLANE, CH), BF)
            halo.edge[side, NONE] = jnp.zeros((16, CH), BF)
            end = (1 - side) * (EDGE - 1)
            faces = field[end * EDGE : (end + 1) * EDGE].astype(F32).reshape(EDGE, 2, EDGE, CH)
            walls = jnp.stack([field[p * EDGE + end].astype(F32) for p in range(EDGE)], 0)
            walls = walls.reshape(EDGE, 2, EDGE, CH)
            face = [faces[:, b].reshape(PLANE, CH) for b in range(2)]
            wall = [walls[:, b].reshape(PLANE, CH) for b in range(2)]
            for b in range(2):
                halo.face[side, b] = face[b].astype(BF)
                halo.wall[side, b] = wall[b].astype(BF)
                ends = jnp.concatenate([face[b][:EDGE], face[b][PLANE - EDGE :]], 0)
                halo.edge[side, b] = ends.astype(BF)
            chosen = []
            for r in range(2):
                for listed, picks in ((sx, face), (sy, wall)):
                    slot = listed[side, r]
                    low = jnp.where(slot == 0, picks[0], 0.0)
                    chosen.append(jnp.where(slot == 1, picks[1], low))
            for r in range(2):
                halo.face_out[side, r] = chosen[2 * r].astype(BF)
                halo.wall_out[side, r] = chosen[2 * r + 1].astype(BF)
            tops = jnp.concatenate([chosen[2 * r + 1][PLANE - EDGE :] for r in range(2)], 0)
            bottoms = jnp.concatenate([chosen[2 * r + 1][:EDGE] for r in range(2)], 0)
            halo.diag_out[0, side] = tops.astype(BF)
            halo.diag_out[1, side] = bottoms.astype(BF)

    def halo_copies(n, halo):
        copies = []

        def add(src, dst, who):
            m = len(copies)
            copies.append(remote(src, dst, halo_s.at[n, m], halo_r.at[n, m], who))

        for d in range(2):
            add(halo.wall_out.at[d], halo.wall.at[d, 2 + 2 * d : 4 + 2 * d], (gx, near_y[d]))
        for d in range(2):
            for e in range(2):
                add(halo.diag_out.at[d, e], halo.diag.at[d, e], (near_x[d], near_y[e]))
        for d in range(2):
            add(halo.face_out.at[d], halo.face.at[d, 6 + 6 * d : 8 + 6 * d], (near_x[d], gy))
        if n == 0:
            for d in range(2):
                add(list_out.at[d], lists.at[d], (near_x[d], gy))
        return copies

    def far_edges(halo):
        blank = jnp.zeros((EDGE, CH), F32)
        for r in range(2, 6):
            got = halo.wall[(r - 2) // 2, r].astype(F32)
            for side, part in ((0, got[PLANE - EDGE :]), (1, got[:EDGE])):
                pair = [blank, part] if r < 4 else [part, blank]
                halo.edge[side, r] = jnp.concatenate(pair, 0).astype(BF)
        for side in range(2):
            below = halo.diag[side, 0].astype(F32)
            above = halo.diag[side, 1].astype(F32)
            table = lists[side].astype(F32)
            for r in range(6):
                row = jnp.broadcast_to(table[r : r + 1], (EDGE, CH))
                low, high = blank, blank
                if r < 2:
                    got = halo.face[side, 6 + 6 * side + r].astype(F32)
                    low, high = got[:EDGE], got[PLANE - EDGE :]
                for i in range(2):
                    part = slice(i * EDGE, (i + 1) * EDGE)
                    high = jnp.where(row == 2.0 + i, below[part], high)
                    low = jnp.where(row == 4.0 + i, above[part], low)
                halo.edge[side, 6 + 6 * side + r] = jnp.concatenate([low, high], 0).astype(BF)

    def inner(field, z_ref, f):
        linked = [[(nbr[b, 12 + 2 * d] != NONE).astype(F32) for b in range(2)] for d in range(2)]

        def layer(p, carry):
            own = field[pl.ds(p * EDGE, EDGE)].astype(F32).reshape(EDGE, 2, EDGE, CH)
            near = [jnp.stack([own[:, 1] * linked[d][0], own[:, 0] * linked[d][1]], 1) for d in range(2)]
            for e, rows in enumerate(with_z(own, *near)):
                z_ref[f, p + 1, 1 : EDGE + 1, :, e * CH : (e + 1) * CH] = rows
            return carry

        lax.fori_loop(0, EDGE, layer, 0)

    def shell(halo, z_ref, f):
        far_edges(halo)

        def three(first, load):
            pick = lambda k: jnp.stack([load(nbr[b, k]).astype(F32) for b in range(2)], 1)
            return pick(first + 1), pick(first), pick(first + 2)

        middle = slice(1, EDGE + 1)
        for side in range(2):
            end = (EDGE + 1) * side
            faces = three(18 * side + 3, lambda r: halo.face[side, r].reshape(EDGE, EDGE, CH))
            for e, rows in enumerate(with_z(*faces)):
                z_ref[f, end, middle, :, e * CH : (e + 1) * CH] = rows
            walls = three(
                9 + 6 * side, lambda r: halo.wall[side, jnp.minimum(r, 6)].reshape(EDGE, EDGE, CH)
            )
            for e, rows in enumerate(with_z(*walls)):
                z_ref[f, middle, end, :, e * CH : (e + 1) * CH] = rows
            for up in range(2):
                low = (1 - up) * EDGE
                lines = three(
                    18 * side + 6 * up,
                    lambda r: halo.edge[side, r].astype(F32)[low : low + EDGE].reshape(1, EDGE, CH),
                )
                for e, rows in enumerate(with_z(*lines)):
                    z_ref[f, end, (EDGE + 1) * up, :, e * CH : (e + 1) * CH] = rows[0]

    half = 2
    tiles = half * EDGE
    steps = EDGE // half
    taps = [(a, c) for a in range(3) for c in range(3)]

    def columns(z_ref, f, m):
        parts = [
            z_ref[f, pl.ds(m * half + a, half), c : c + EDGE].reshape(tiles * 16, 3 * CH) for a, c in taps
        ]
        return jnp.concatenate(parts, 1)

    def conv(z_ref, f, m, w):
        return jnp.dot(columns(z_ref, f, m), w[...], preferred_element_type=F32)

    def conv_t(z_ref, f, m, w):
        turned = jnp.concatenate([w[(KVOL - 1 - k) * CH : (KVOL - k) * CH] for k in range(KVOL)], 1)
        return lax.dot_general(
            columns(z_ref, f, m), turned, (((1,), (1,)), ((), ())), preferred_element_type=F32
        )

    for d in range(2):
        index = lax.broadcasted_iota(jnp.int32, (16, CH), 0)
        table = jnp.full((16, CH), float(NONE), F32)
        for r in range(6):
            table = jnp.where(index == r, sx[d, r].astype(F32), table)
        list_out[d] = table.astype(BF)
    own_faces(fa0, halos[0])
    own_faces(fa1, halos[1])
    copies = [halo_copies(n, halos[n]) for n in range(4)]
    pl.semaphore_wait(barrier, len(greet))
    for copy in copies[0] + copies[1]:
        copy.start()
    inner(fa0, za, 0)
    inner(fa1, za, 1)
    load_w1.wait()
    load_w2.wait()
    for copy in copies[0]:
        copy.wait()
    shell(halos[0], za, 0)

    def forward_layer(m, carry):
        part = pl.ds(m * tiles, tiles)
        mk = mask[part].reshape(tiles * 16, CH)
        preact = conv(za, 0, m, w1) + bias[...]
        hidden = (jnp.maximum(preact, 0.0) * mk).astype(BF)
        gate[part] = jnp.where(preact > 0, mk, 0.0).reshape(tiles, 16, CH)
        fb0[part] = hidden.reshape(tiles, 16, CH)
        at[1, m] = hidden.T
        return carry

    lax.fori_loop(0, steps, forward_layer, 0)
    own_faces(fb0, halos[2])
    for copy in copies[1]:
        copy.wait()
    for copy in copies[2]:
        copy.start()
    shell(halos[1], za, 1)

    def backward_layer(m, carry):
        part = pl.ds(m * tiles, tiles)
        grad = (conv_t(za, 1, m, w2) * gate[part].reshape(tiles * 16, CH)).astype(BF)
        fb1[part] = grad.reshape(tiles, 16, CH)
        at[0, m] = grad.T
        return carry

    lax.fori_loop(0, steps, backward_layer, 0)
    own_faces(fb1, halos[3])
    for copy in copies[3]:
        copy.start()

    third = 9 * CH

    def weight_grad(which, a, dst, add=None):
        left = jnp.concatenate([at[which, i] for i in range(steps)], 1)
        first = which == 0
        pa = jnp.where(first, a, 2 - a)
        for c in range(3):
            pc = jnp.where(first, c, 2 - c)
            right = za[which, pl.ds(pa, EDGE), pl.ds(pc, EDGE)].reshape(PLANE * 16, 3 * CH)
            prod = jnp.dot(left, right, preferred_element_type=F32)
            for e in range(3):
                plain = prod[:, (2 - e) * CH : (3 - e) * CH]
                turned = prod[:, e * CH : (e + 1) * CH].T
                block = jnp.where(first, turned, plain)
                row = (9 * a + 3 * c + e) * CH
                if add is not None:
                    block = block + add[row : row + CH].astype(F32)
                dst[row : row + CH] = block.astype(BF)

    core_copies = [
        remote(
            gwo.at[a * third : (a + 1) * third],
            crecv.at[a * third : (a + 1) * third],
            core_s.at[a],
            core_r.at[a],
            partner,
        )
        for a in range(3)
    ]
    for a in range(3):
        weight_grad(1 - core, a, gwo)
        core_copies[a].start()
    part_q = Part(remote, gwm, gw_ref, 0, third, line, plane, bufs_q, sems_q)
    part_p = Part(remote, gwm, gw_ref, third, 2 * third, plane, line, bufs_p, sems_p)
    for a in range(3):
        core_copies[a].wait()
        weight_grad(core, a, gwm, crecv)
        if a == 0:
            part_q.scatter_one()
    part_p.scatter_one()
    inner(fb0, zb, 0)
    inner(fb1, zb, 1)
    part_q.scatter_two()
    part_p.scatter_two()

    def write(value, dst, m):
        rows = pl.ds(pl.multiple_of(m * tiles * EDGE, tiles * EDGE), tiles * EDGE)
        bricks = value.reshape(tiles, 2, EDGE, CH)
        for b in range(2):
            dst[b, rows] = bricks[:, b].reshape(tiles * EDGE, CH).astype(BF)

    def second_layer(m, carry):
        part = pl.ds(m * tiles, tiles)
        masked = fa0[part].astype(F32).reshape(tiles * 16, CH)
        write(conv(zb, 0, m, w2) * mask[part].reshape(tiles * 16, CH) + masked, out_ref, m)
        return carry

    for copy in copies[2]:
        copy.wait()
    shell(halos[2], zb, 0)
    lax.fori_loop(0, steps, second_layer, 0)
    part_q.gather_two(scale)
    part_p.gather_two(scale)

    def last_layer(m, carry):
        part = pl.ds(m * tiles, tiles)
        given = fa1[part].astype(F32).reshape(tiles * 16, CH)
        write(conv_t(zb, 1, m, w1) * mask[part].reshape(tiles * 16, CH) + given, gf_ref, m)
        return carry

    for copy in copies[3]:
        copy.wait()
    shell(halos[3], zb, 1)
    lax.fori_loop(0, steps, last_layer, 0)
    part_q.gather_one(core, partner)
    part_p.gather_one(core, partner)
    for step in range(max(plane.size, line.size) - 1):
        for part in (part_q, part_p):
            if step < part.first.size - 1:
                part.finish(core, partner, step)
    for part in (part_q, part_p):
        for copy in part.passed:
            copy.wait()


def convert(out_in, gf_in, gw_in, out, gf, one, two):
    out[...] = out_in[...]
    gf[...] = gf_in[...]
    one[...] = gw_in[0].astype(F32)
    two[...] = gw_in[1].astype(F32)


def on_device(dims, features, occupied, weight_one, bias_one, weight_two, cotangent, neighbours, send_x, send_y):
    nx, ny, nzhi, nzlo, _ = dims
    nz, nxy = nzhi * nzlo, nx * ny
    slots, voxels, _ = features.shape
    scale = 1.0 / math.sqrt(slots * voxels * 2 * nxy * nz)
    vmem = pl.BlockSpec(memory_space=pltpu.VMEM)
    smem = pl.BlockSpec(memory_space=pltpu.SMEM)
    hbm = pl.BlockSpec(memory_space=pl.ANY)
    rows = KVOL * CH

    def halo():
        return [
            pltpu.VMEM((2, NONE + 1, PLANE, CH), BF),
            pltpu.VMEM((2, 7, PLANE, CH), BF),
            pltpu.VMEM((2, NONE + 1, 16, CH), BF),
            pltpu.VMEM((2, 2, PLANE, CH), BF),
            pltpu.VMEM((2, 2, PLANE, CH), BF),
            pltpu.VMEM((2, 2, 16, CH), BF),
            pltpu.VMEM((2, 2, 16, CH), BF),
        ]

    sem = lambda *shape: pltpu.SemaphoreType.DMA(shape)

    def part(total, n_one, n_two):
        one = total // n_one
        two = -(-one // (16 * n_two)) * 16
        bufs = [
            pltpu.VMEM((n_one, one, CH), BF),
            pltpu.VMEM((n_two * two, CH), BF),
            pltpu.VMEM((n_two, two, CH), BF),
            pltpu.VMEM((n_two * two, CH), BF),
        ]
        sizes = (n_one, n_one, n_two, n_two, n_two, n_two, n_one, n_one, n_one, n_one)
        return bufs, [sem(n) for n in sizes]

    bufs_q, sems_q = part(rows // 3, nz, nxy)
    bufs_p, sems_p = part(2 * rows // 3, nxy, nz)
    field = pltpu.VMEM((PLANE, 16, CH), BF)
    weight = pltpu.VMEM((rows, CH), BF)
    plain = pltpu.VMEM((PLANE, 16, CH), F32)
    padded = pltpu.VMEM((2, EDGE + 2, EDGE + 2, 16, 3 * CH), BF)
    lists = pltpu.VMEM((2, 16, CH), BF)
    made = pl.pallas_call(
        functools.partial(kernel, dims, scale),
        out_shape=(
            jax.ShapeDtypeStruct(features.shape, BF),
            jax.ShapeDtypeStruct(features.shape, BF),
            jax.ShapeDtypeStruct((2, rows, CH), BF),
        ),
        in_specs=[vmem, vmem, hbm, vmem, hbm, vmem, smem, smem, smem],
        out_specs=(vmem, vmem, vmem),
        scratch_shapes=[
            weight, weight, plain, plain, field, field, field, field, padded, padded,
            pltpu.VMEM((2, 4, CH, 256), BF),
            lists, lists, weight, weight, weight,
            *halo(), *halo(), *halo(), *halo(),
            *bufs_q, *bufs_p,
            sem(2), sem(4, 10), sem(4, 10), sem(3), sem(3),
            *sems_q, *sems_p,
        ],
        compiler_params=pltpu.CompilerParams(
            collective_id=0, has_side_effects=True, vmem_limit_bytes=56 * 2**20
        ),
    )(
        features,
        occupied,
        weight_one.reshape(rows, CH),
        bias_one.reshape(1, CH),
        weight_two.reshape(rows, CH),
        cotangent,
        neighbours,
        send_x.reshape(2, -1),
        send_y.reshape(2, -1),
    )
    cuts = 4
    brick = pl.BlockSpec((slots, voxels // cuts, CH), lambda i: (0, i, 0))
    grad = pl.BlockSpec((rows // cuts, CH), lambda i: (i, 0))
    out, grad_features, one, two = pl.pallas_call(
        convert,
        grid=(cuts,),
        out_shape=(
            jax.ShapeDtypeStruct(features.shape, BF),
            jax.ShapeDtypeStruct(features.shape, BF),
            jax.ShapeDtypeStruct((rows, CH), F32),
            jax.ShapeDtypeStruct((rows, CH), F32),
        ),
        in_specs=[brick, brick, pl.BlockSpec((2, rows // cuts, CH), lambda i: (0, i, 0))],
        out_specs=(brick, brick, grad, grad),
        compiler_params=pltpu.CompilerParams(vmem_limit_bytes=24 * 2**20),
    )(*made)
    return (out, grad_features, one.reshape(KVOL, CH, CH), two.reshape(KVOL, CH, CH))


def solution(mesh, dims=SLICE):
    in_specs = (
        P(("gx", "gy"), None, None),
        P(("gx", "gy"), None),
        P(),
        P(),
        P(),
        P(("gx", "gy"), None, None),
        P(("gx", "gy"), None),
        P(("gx", "gy"), None, None),
        P(("gx", "gy"), None, None),
    )
    out_specs = (P(("gx", "gy"), None, None), P(("gx", "gy"), None, None), P(), P())
    return jax.shard_map(
        functools.partial(on_device, dims), mesh=mesh, in_specs=in_specs, out_specs=out_specs, check_vma=False
    )
```

time: 89.5 us -> 74 us (0.83)
  Pallas kernels: 82.9 us -> 69.8 us
  other arithmetic: 2.81 us -> 0 us
    pallas_call x1, Pallas kernels: 82.9 us -> 67.2 us  [on_device(): pl.pallas_call(functools.partial(kernel, dims, scale), out_shape=(jax.Sha...]
    convert_element_type x2 -> x0, other arithmetic: 2.81 us -> none  [on_device(): grads[j, :rows].astype(F32).reshape(KVOL, CH, CH)]
    pallas_call x0 -> x1, Pallas kernels: none -> 2.53 us  [on_device(): pl.pallas_call(convert, grid=(cuts,), out_shape=(jax.ShapeDtypeStruct(fea...]
    unnamed x6, local copies, waits for them, and re-layouts: 1.41 us -> 3.37 us
    slice x1 -> x0, local copies, waits for them, and re-layouts: 1.55 us -> none  [on_device(): grads[j, :rows].astype(F32).reshape(KVOL, CH, CH)]
where the time goes in v2:
time: 74 us; the launch traced here: 73.8 us
  Pallas kernels  69.8 us (94%)
  local copies, waits for them, and re-layouts  3.37 us (5%)
    pallas_call x1, Pallas kernels, on_device(): pl.pallas_call(functools.partial(kernel, dims, scale), out_shape=(jax.Sha...  67.2 us
    unnamed x6, local copies, waits for them, and re-layouts  3.37 us
    pallas_call x1, Pallas kernels, on_device(): pl.pallas_call(convert, grid=(cuts,), out_shape=(jax.ShapeDtypeStruct(fea...  2.53 us

profile of v2, /device:TPU:1, one launch (start us, length us, event | category | flops | bytes accessed | tf_op | source)
XLA Modules:
  0.0 73.8 jit_solution(10181057086709363210)
XLA Ops:
  0.6 67.2 %shard_map.120 = (bf16[2,512,128]{2,1,0:T(8,128)(2,1)}, bf16[2,512,128]{2,1,0:T(8,128)(2,1)}, bf16[2,3456,128]{2,1,0:T(8,128)(2,1)}) custom-call(bf16[2,512,128]{2,1,0:T(8,128)(2,1)} %refs_0_.1, s32[2,512]{1,0:T(2,128)} %refs_1_.1, bf16[3456,128]{1,0:T(8,128)(2,1)} %bitcast.7, f32[1,128]{1,0:T(1,128)} %bitcast.11, bf16[3456,128]{1,0:T(8,128)(2,1)} %bitcast.8, ...), custom_call_target="tpu_custom_call" | custom-call | tf_op jit(solution)/shard_map/pallas_call | solution.py:514
  67.9 0.0 copy-start
  67.9 1.5 %copy-done = bf16[2,3456,128]{2,1,0:T(8,128)(2,1)S(1)} copy-done((bf16[2,3456,128]{2,1,0:T(8,128)(2,1)S(1)}, bf16[2,3456,128]{2,1,0:T(8,128)(2,1)}, u32[]{:S(2)}) %copy-start) | copy-done | bytes 1769496
  69.3 0.0 copy-start.1
  69.3 0.9 %copy-done.1 = bf16[2,512,128]{2,1,0:T(8,128)(2,1)S(1)} copy-done((bf16[2,512,128]{2,1,0:T(8,128)(2,1)S(1)}, bf16[2,512,128]{2,1,0:T(8,128)(2,1)}, u32[]{:S(2)}) %copy-start.1) | copy-done | bytes 262168
  70.3 0.0 copy-start.2
  70.3 0.9 %copy-done.2 = bf16[2,512,128]{2,1,0:T(8,128)(2,1)S(1)} copy-done((bf16[2,512,128]{2,1,0:T(8,128)(2,1)S(1)}, bf16[2,512,128]{2,1,0:T(8,128)(2,1)}, u32[]{:S(2)}) %copy-start.2) | copy-done | bytes 262168
  71.2 2.5 %shard_map.121 = (bf16[2,512,128]{2,1,0:T(8,128)(2,1)}, bf16[2,512,128]{2,1,0:T(8,128)(2,1)}, f32[3456,128]{1,0:T(8,128)}, f32[3456,128]{1,0:T(8,128)}) custom-call(bf16[2,512,128]{2,1,0:T(8,128)(2,1)S(1)} %copy-done.1, bf16[2,512,128]{2,1,0:T(8,128)(2,1)S(1)} %copy-done.2, bf16[2,3456,128]{2,1,0:T(8,128)(2,1)S(1)} %copy-done), custom_call_target="tpu_custom_call" | custom-call | tf_op jit(solution)/shard_map/pallas_call | solution.py:549
Async XLA Ops:
  67.9 1.5 %copy-start = (bf16[2,3456,128]{2,1,0:T(8,128)(2,1)S(1)}, bf16[2,3456,128]{2,1,0:T(8,128)(2,1)}, u32[]{:S(2)}) copy-start(bf16[2,3456,128]{2,1,0:T(8,128)(2,1)} %get-tuple-element.13.gw_in) | copy-start | bytes 5308420
  69.3 0.9 %copy-start.1 = (bf16[2,512,128]{2,1,0:T(8,128)(2,1)S(1)}, bf16[2,512,128]{2,1,0:T(8,128)(2,1)}, u32[]{:S(2)}) copy-start(bf16[2,512,128]{2,1,0:T(8,128)(2,1)} %get-tuple-element.11.out_in) | copy-start | bytes 786436
  70.3 0.9 %copy-start.2 = (bf16[2,512,128]{2,1,0:T(8,128)(2,1)S(1)}, bf16[2,512,128]{2,1,0:T(8,128)(2,1)}, u32[]{:S(2)}) copy-start(bf16[2,512,128]{2,1,0:T(8,128)(2,1)} %get-tuple-element.12.gf_in) | copy-start | bytes 786436

commit v3 on v2

--- a/solution.py
+++ b/solution.py
@@ -124,8 +124,9 @@
     (
         feat, occ, w1_hbm, bias, w2_hbm, cot, nbr, sx, sy,
         out_ref, gf_ref, gw_ref,
-        w1, w2, mask, gate, fa0, fa1, fb0, fb1, za, zb, at, list_out, lists, gwo, gwm, crecv,
-    ) = refs[:28]
+        w1, w2, mask, gate, sum0, sum1, fa0, fa1, fb0, fb1, za, zb, at, list_out, lists, gwo, gwm, crecv,
+    ) = refs[:30]
+    refs = refs[2:]
     halos = [Halo(refs[28 + 7 * i : 35 + 7 * i]) for i in range(4)]
     bufs_q, bufs_p = refs[56:60], refs[60:64]
     w_sem, halo_s, halo_r, core_s, core_r = refs[64:69]
@@ -178,18 +179,17 @@
             halves.append(jnp.broadcast_to(row, (CH, CH)).T.reshape(16, EDGE, CH))
         mask[t * 16 : (t + 1) * 16] = jnp.stack(halves, 1).reshape(16, 16, CH)
 
-    def fields(p, carry):
-        part = pl.ds(p * EDGE, EDGE)
-        mk = mask[part]
-        rows = pl.ds(pl.multiple_of(p * PLANE, PLANE), PLANE)
-        for source, field in ((feat, fa0), (cot, fa1)):
+    def masked_field(source, field):
+        def layer(p, carry):
+            part = pl.ds(p * EDGE, EDGE)
+            rows = pl.ds(pl.multiple_of(p * PLANE, PLANE), PLANE)
             both = jnp.stack(
                 [source[b, rows].astype(F32).reshape(EDGE, EDGE, CH) for b in range(2)], 1
             )
-            field[part] = (both.reshape(EDGE, 16, CH) * mk).astype(BF)
-        return carry
-
-    lax.fori_loop(0, EDGE, fields, 0)
+            field[part] = (both.reshape(EDGE, 16, CH) * mask[part]).astype(BF)
+            return carry
+
+        lax.fori_loop(0, EDGE, layer, 0)
 
     def remote(src, dst, send, recv, who):
         return pltpu.make_async_remote_copy(
@@ -333,24 +333,79 @@
         for r in range(6):
             table = jnp.where(index == r, sx[d, r].astype(F32), table)
         list_out[d] = table.astype(BF)
+    masked_field(feat, fa0)
     own_faces(fa0, halos[0])
-    own_faces(fa1, halos[1])
     copies = [halo_copies(n, halos[n]) for n in range(4)]
     pl.semaphore_wait(barrier, len(greet))
-    for copy in copies[0] + copies[1]:
+    for copy in copies[0]:
         copy.start()
+    masked_field(cot, fa1)
+    own_faces(fa1, halos[1])
+    for copy in copies[1]:
+        copy.start()
+
+    for f in range(2):
+        for end in (0, EDGE + 1):
+            za[f, end] = jnp.zeros((EDGE + 2, 16, 3 * CH), BF)
+            za[f, 1 : EDGE + 1, end] = jnp.zeros((EDGE, 16, 3 * CH), BF)
     inner(fa0, za, 0)
+    load_w1.wait()
+
+    def inside_forward(m, carry):
+        sum0[pl.ds(m * tiles, tiles)] = conv(za, 0, m, w1).reshape(tiles, 16, CH)
+        return carry
+
+    lax.fori_loop(0, steps, inside_forward, 0)
     inner(fa1, za, 1)
-    load_w1.wait()
     load_w2.wait()
+
+    def inside_backward(m, carry):
+        sum1[pl.ds(m * tiles, tiles)] = conv_t(za, 1, m, w2).reshape(tiles, 16, CH)
+        return carry
+
+    lax.fori_loop(0, steps, inside_backward, 0)
+
+    def sides(f, w, total, turned):
+        def times(parts, which):
+            left = jnp.concatenate([t.reshape(EDGE * 16, 3 * CH) for t in parts], 1)
+            if turned:
+                blocks = [
+                    w[(KVOL - 1 - k) * CH : (KVOL - k) * CH]
+                    for a, c in which
+                    for k in range(9 * a + 3 * c, 9 * a + 3 * c + 3)
+                ]
+                right = jnp.concatenate(blocks, 1)
+                got = lax.dot_general(left, right, (((1,), (1,)), ((), ())), preferred_element_type=F32)
+            else:
+                right = jnp.concatenate([w[(3 * a + c) * 3 * CH : (3 * a + c + 1) * 3 * CH] for a, c in which], 0)
+                got = jnp.dot(left, right, preferred_element_type=F32)
+            return got.reshape(EDGE, 16, CH)
+
+        none = jnp.zeros((1, 16, 3 * CH), BF)
+        for side in range(2):
+            shell_at, inner_at, tap = (EDGE + 1) * side, (EDGE - 1) * side, 2 * side
+            parts = [za[f, shell_at, c : c + EDGE] for c in range(3)]
+            rows = slice(inner_at * EDGE, (inner_at + 1) * EDGE)
+            total[rows] = total[rows] + times(parts, [(tap, c) for c in range(3)])
+            wall = za[f, 1 : EDGE + 1, shell_at]
+            parts = [
+                jnp.concatenate([none, wall[: EDGE - 1]], 0),
+                wall,
+                jnp.concatenate([wall[1:], none], 0),
+            ]
+            more = times(parts, [(a, tap) for a in range(3)])
+            for p in range(EDGE):
+                total[p * EDGE + inner_at] = total[p * EDGE + inner_at] + more[p]
+
     for copy in copies[0]:
         copy.wait()
     shell(halos[0], za, 0)
+    sides(0, w1, sum0, False)
 
     def forward_layer(m, carry):
         part = pl.ds(m * tiles, tiles)
         mk = mask[part].reshape(tiles * 16, CH)
-        preact = conv(za, 0, m, w1) + bias[...]
+        preact = sum0[part].reshape(tiles * 16, CH) + bias[...]
         hidden = (jnp.maximum(preact, 0.0) * mk).astype(BF)
         gate[part] = jnp.where(preact > 0, mk, 0.0).reshape(tiles, 16, CH)
         fb0[part] = hidden.reshape(tiles, 16, CH)
@@ -358,24 +413,19 @@
         return carry
 
     lax.fori_loop(0, steps, forward_layer, 0)
-    own_faces(fb0, halos[2])
     for copy in copies[1]:
         copy.wait()
-    for copy in copies[2]:
-        copy.start()
     shell(halos[1], za, 1)
+    sides(1, w2, sum1, True)
 
     def backward_layer(m, carry):
         part = pl.ds(m * tiles, tiles)
-        grad = (conv_t(za, 1, m, w2) * gate[part].reshape(tiles * 16, CH)).astype(BF)
+        grad = (sum1[part] * gate[part]).reshape(tiles * 16, CH).astype(BF)
         fb1[part] = grad.reshape(tiles, 16, CH)
         at[0, m] = grad.T
         return carry
 
     lax.fori_loop(0, steps, backward_layer, 0)
-    own_faces(fb1, halos[3])
-    for copy in copies[3]:
-        copy.start()
 
     third = 9 * CH
 
@@ -417,6 +467,12 @@
         if a == 0:
             part_q.scatter_one()
     part_p.scatter_one()
+    own_faces(fb0, halos[2])
+    for copy in copies[2]:
+        copy.start()
+    own_faces(fb1, halos[3])
+    for copy in copies[3]:
+        copy.start()
     inner(fb0, zb, 0)
     inner(fb1, zb, 1)
     part_q.scatter_two()
@@ -521,7 +577,7 @@
         in_specs=[vmem, vmem, hbm, vmem, hbm, vmem, smem, smem, smem],
         out_specs=(vmem, vmem, vmem),
         scratch_shapes=[
-            weight, weight, plain, plain, field, field, field, field, padded, padded,
+            weight, weight, plain, plain, plain, plain, field, field, field, field, padded, padded,
             pltpu.VMEM((2, 4, CH, 256), BF),
             lists, lists, weight, weight, weight,
             *halo(), *halo(), *halo(), *halo(),
@@ -557,7 +613,7 @@
         ),
         in_specs=[brick, brick, pl.BlockSpec((2, rows // cuts, CH), lambda i: (0, i, 0))],
         out_specs=(brick, brick, grad, grad),
-        compiler_params=pltpu.CompilerParams(vmem_limit_bytes=24 * 2**20),
+        compiler_params=pltpu.CompilerParams(vmem_limit_bytes=60 * 2**20),
     )(*made)
     return (out, grad_features, one.reshape(KVOL, CH, CH), two.reshape(KVOL, CH, CH))
 

time: 74 us -> 75.5 us (1.020)
  Pallas kernels: 69.8 us -> 74.7 us
  local copies, waits for them, and re-layouts: 3.37 us -> 0 us
    unnamed x6 -> x0, local copies, waits for them, and re-layouts: 3.37 us -> none
    pallas_call x1, Pallas kernels: 67.2 us -> 70.4 us  [on_device(): pl.pallas_call(functools.partial(kernel, dims, scale), out_shape=(jax.Sha...]
    pallas_call x1, Pallas kernels: 2.53 us -> 4.25 us  [on_device(): pl.pallas_call(convert, grid=(cuts,), out_shape=(jax.ShapeDtypeStruct(fea...]
where the time goes in v3:
time: 75.5 us; the launch traced here: 75.3 us
  Pallas kernels  74.7 us (99%)
    pallas_call x1, Pallas kernels, on_device(): pl.pallas_call(functools.partial(kernel, dims, scale), out_shape=(jax.Sha...  70.4 us
    pallas_call x1, Pallas kernels, on_device(): pl.pallas_call(convert, grid=(cuts,), out_shape=(jax.ShapeDtypeStruct(fea...  4.25 us

profile of v3, /device:TPU:1, one launch (start us, length us, event | category | flops | bytes accessed | tf_op | source)
XLA Modules:
  0.0 75.3 jit_solution(18386642698268830255)
XLA Ops:
  0.6 70.4 %shard_map.120 = (bf16[2,512,128]{2,1,0:T(8,128)(2,1)}, bf16[2,512,128]{2,1,0:T(8,128)(2,1)}, bf16[2,3456,128]{2,1,0:T(8,128)(2,1)}) custom-call(bf16[2,512,128]{2,1,0:T(8,128)(2,1)} %refs_0_.1, s32[2,512]{1,0:T(2,128)} %refs_1_.1, bf16[3456,128]{1,0:T(8,128)(2,1)} %bitcast.7, f32[1,128]{1,0:T(1,128)} %bitcast.11, bf16[3456,128]{1,0:T(8,128)(2,1)} %bitcast.8, ...), custom_call_target="tpu_custom_call" | custom-call | tf_op jit(solution)/shard_map/pallas_call | solution.py:570
  71.1 4.2 %shard_map.121 = (bf16[2,512,128]{2,1,0:T(8,128)(2,1)}, bf16[2,512,128]{2,1,0:T(8,128)(2,1)}, f32[3456,128]{1,0:T(8,128)}, f32[3456,128]{1,0:T(8,128)}) custom-call(bf16[2,512,128]{2,1,0:T(8,128)(2,1)} %get-tuple-element.11.out_in, bf16[2,512,128]{2,1,0:T(8,128)(2,1)} %get-tuple-element.12.gf_in, bf16[2,3456,128]{2,1,0:T(8,128)(2,1)} %get-tuple-element.13.gw_in), custom_call_target="tpu_custom_call" | custom-call | tf_op jit(solution)/shard_map/pallas_call | solution.py:605

commit v4 on v3

--- a/solution.py
+++ b/solution.py
@@ -413,6 +413,9 @@
         return carry
 
     lax.fori_loop(0, steps, forward_layer, 0)
+    own_faces(fb0, halos[2])
+    for copy in copies[2]:
+        copy.start()
     for copy in copies[1]:
         copy.wait()
     shell(halos[1], za, 1)
@@ -426,6 +429,9 @@
         return carry
 
     lax.fori_loop(0, steps, backward_layer, 0)
+    own_faces(fb1, halos[3])
+    for copy in copies[3]:
+        copy.start()
 
     third = 9 * CH
 
@@ -467,12 +473,6 @@
         if a == 0:
             part_q.scatter_one()
     part_p.scatter_one()
-    own_faces(fb0, halos[2])
-    for copy in copies[2]:
-        copy.start()
-    own_faces(fb1, halos[3])
-    for copy in copies[3]:
-        copy.start()
     inner(fb0, zb, 0)
     inner(fb1, zb, 1)
     part_q.scatter_two()
@@ -518,11 +518,20 @@
             copy.wait()
 
 
-def convert(out_in, gf_in, gw_in, out, gf, one, two):
-    out[...] = out_in[...]
-    gf[...] = gf_in[...]
-    one[...] = gw_in[0].astype(F32)
-    two[...] = gw_in[1].astype(F32)
+def convert(out_in, gf_in, gw_in, out, gf, one, two, wide, sems):
+    copies = [pltpu.make_async_copy(out_in, out, sems.at[0]), pltpu.make_async_copy(gf_in, gf, sems.at[1])]
+    for copy in copies:
+        copy.start()
+    cuts = 3
+    size = gw_in.shape[1] // cuts
+    for j, dst in enumerate((one, two)):
+        for i in range(cuts):
+            rows = pl.ds(i * size, size)
+            wide[j, rows] = gw_in[j, rows].astype(F32)
+            copies.append(pltpu.make_async_copy(wide.at[j, rows], dst.at[rows], sems.at[len(copies)]))
+            copies[-1].start()
+    for copy in copies:
+        copy.wait()
 
 
 def on_device(dims, features, occupied, weight_one, bias_one, weight_two, cotangent, neighbours, send_x, send_y):
@@ -570,9 +579,9 @@
     made = pl.pallas_call(
         functools.partial(kernel, dims, scale),
         out_shape=(
-            jax.ShapeDtypeStruct(features.shape, BF),
-            jax.ShapeDtypeStruct(features.shape, BF),
-            jax.ShapeDtypeStruct((2, rows, CH), BF),
+            pltpu.VMEM(features.shape, BF),
+            pltpu.VMEM(features.shape, BF),
+            pltpu.VMEM((2, rows, CH), BF),
         ),
         in_specs=[vmem, vmem, hbm, vmem, hbm, vmem, smem, smem, smem],
         out_specs=(vmem, vmem, vmem),
@@ -599,21 +608,18 @@
         send_x.reshape(2, -1),
         send_y.reshape(2, -1),
     )
-    cuts = 4
-    brick = pl.BlockSpec((slots, voxels // cuts, CH), lambda i: (0, i, 0))
-    grad = pl.BlockSpec((rows // cuts, CH), lambda i: (i, 0))
     out, grad_features, one, two = pl.pallas_call(
         convert,
-        grid=(cuts,),
         out_shape=(
             jax.ShapeDtypeStruct(features.shape, BF),
             jax.ShapeDtypeStruct(features.shape, BF),
             jax.ShapeDtypeStruct((rows, CH), F32),
             jax.ShapeDtypeStruct((rows, CH), F32),
         ),
-        in_specs=[brick, brick, pl.BlockSpec((2, rows // cuts, CH), lambda i: (0, i, 0))],
-        out_specs=(brick, brick, grad, grad),
-        compiler_params=pltpu.CompilerParams(vmem_limit_bytes=60 * 2**20),
+        in_specs=[vmem, vmem, vmem],
+        out_specs=(hbm, hbm, hbm, hbm),
+        scratch_shapes=[pltpu.VMEM((2, rows, CH), F32), sem(8)],
+        compiler_params=pltpu.CompilerParams(vmem_limit_bytes=24 * 2**20),
     )(*made)
     return (out, grad_features, one.reshape(KVOL, CH, CH), two.reshape(KVOL, CH, CH))
 

time: 75.5 us -> 66.1 us (0.88)
  Pallas kernels: 74.7 us -> 65.4 us
    pallas_call x2, Pallas kernels: 74.7 us -> 65.4 us  [the longest x1 63.4 us: on_device(): pl.pallas_call(functools.partial(kernel, dims, scale), out_shape=(pltpu.V...]
where the time goes in v4:
time: 66.1 us; the launch traced here: 66 us
  Pallas kernels  65.4 us (99%)
    pallas_call x1, Pallas kernels, on_device(): pl.pallas_call(functools.partial(kernel, dims, scale), out_shape=(pltpu.V...  63.4 us
    pallas_call x1, Pallas kernels, on_device(): pl.pallas_call(convert, out_shape=(jax.ShapeDtypeStruct(features.shape, B...  2.03 us

profile of v4, /device:TPU:1, one launch (start us, length us, event | category | flops | bytes accessed | tf_op | source)
XLA Modules:
  0.0 66.0 jit_solution(743494169239456818)
XLA Ops:
  0.6 63.4 %shard_map.120 = (bf16[2,512,128]{2,1,0:T(8,128)(2,1)S(1)}, bf16[2,512,128]{2,1,0:T(8,128)(2,1)S(1)}, bf16[2,3456,128]{2,1,0:T(8,128)(2,1)S(1)}) custom-call(bf16[2,512,128]{2,1,0:T(8,128)(2,1)} %refs_0_.1, s32[2,512]{1,0:T(2,128)} %refs_1_.1, bf16[3456,128]{1,0:T(8,128)(2,1)} %bitcast.7, f32[1,128]{1,0:T(1,128)} %bitcast.11, bf16[3456,128]{1,0:T(8,128)(2,1)} %bitcast.8, ...), custom_call_target="tpu_custom_call" | custom-call | tf_op jit(solution)/shard_map/pallas_call | solution.py:579
  64.0 2.0 %shard_map.121 = (bf16[2,512,128]{2,1,0:T(8,128)(2,1)}, bf16[2,512,128]{2,1,0:T(8,128)(2,1)}, f32[3456,128]{1,0:T(8,128)}, f32[3456,128]{1,0:T(8,128)}) custom-call(bf16[2,512,128]{2,1,0:T(8,128)(2,1)S(1)} %get-tuple-element.11.out_in, bf16[2,512,128]{2,1,0:T(8,128)(2,1)S(1)} %get-tuple-element.12.gf_in, bf16[2,3456,128]{2,1,0:T(8,128)(2,1)S(1)} %get-tuple-element.13.gw_in), custom_call_target="tpu_custom_call" | custom-call | tf_op jit(solution)/shard_map/pallas_call | solution.py:611

commit v5 on v4

--- a/solution.py
+++ b/solution.py
@@ -153,11 +153,14 @@
                 px, py = lax.rem(x + i, nx), lax.rem(y + k, ny)
                 back = lax.rem(x + nx - i, nx) * ny + lax.rem(y + ny - k, ny)
                 in_plane.append((i * ny + k, device(px, py, z, core), px * ny + py, back))
+    ring = lambda i, n: min(i, n - i)
+    in_plane.sort(key=lambda p: -(ring(p[0] // ny, nx) + ring(p[0] % ny, ny)))
     plane = Group(nx * ny, x * ny + y, in_plane)
     in_line = [
         (d, device(x, y, lax.rem(z + d, nz), core), lax.rem(z + d, nz), lax.rem(z + nz - d, nz))
         for d in range(1, nz)
     ]
+    in_line.sort(key=lambda p: -ring(p[0], nz))
     line = Group(nz, z, in_line)
 
     barrier = pltpu.get_barrier_semaphore()
@@ -512,7 +515,7 @@
     for step in range(max(plane.size, line.size) - 1):
         for part in (part_q, part_p):
             if step < part.first.size - 1:
-                part.finish(core, partner, step)
+                part.finish(core, partner, part.first.size - 2 - step)
     for part in (part_q, part_p):
         for copy in part.passed:
             copy.wait()

time: 66.1 us -> 64.3 us (0.973)
  Pallas kernels: 65.4 us -> 63.6 us
    pallas_call x1, Pallas kernels: 63.4 us -> 61.5 us  [on_device(): pl.pallas_call(functools.partial(kernel, dims, scale), out_shape=(pltpu.V...]
where the time goes in v5:
time: 64.3 us; the launch traced here: 64.2 us
  Pallas kernels  63.6 us (99%)
    pallas_call x1, Pallas kernels, on_device(): pl.pallas_call(functools.partial(kernel, dims, scale), out_shape=(pltpu.V...  61.5 us
    pallas_call x1, Pallas kernels, on_device(): pl.pallas_call(convert, out_shape=(jax.ShapeDtypeStruct(features.shape, B...  2.03 us

profile of v5, /device:TPU:1, one launch (start us, length us, event | category | flops | bytes accessed | tf_op | source)
XLA Modules:
  0.0 64.2 jit_solution(4520261909734789282)
XLA Ops:
  0.6 61.5 %shard_map.120 = (bf16[2,512,128]{2,1,0:T(8,128)(2,1)S(1)}, bf16[2,512,128]{2,1,0:T(8,128)(2,1)S(1)}, bf16[2,3456,128]{2,1,0:T(8,128)(2,1)S(1)}) custom-call(bf16[2,512,128]{2,1,0:T(8,128)(2,1)} %refs_0_.1, s32[2,512]{1,0:T(2,128)} %refs_1_.1, bf16[3456,128]{1,0:T(8,128)(2,1)} %bitcast.7, f32[1,128]{1,0:T(1,128)} %bitcast.11, bf16[3456,128]{1,0:T(8,128)(2,1)} %bitcast.8, ...), custom_call_target="tpu_custom_call" | custom-call | tf_op jit(solution)/shard_map/pallas_call | solution.py:582
  62.2 2.0 %shard_map.121 = (bf16[2,512,128]{2,1,0:T(8,128)(2,1)}, bf16[2,512,128]{2,1,0:T(8,128)(2,1)}, f32[3456,128]{1,0:T(8,128)}, f32[3456,128]{1,0:T(8,128)}) custom-call(bf16[2,512,128]{2,1,0:T(8,128)(2,1)S(1)} %get-tuple-element.11.out_in, bf16[2,512,128]{2,1,0:T(8,128)(2,1)S(1)} %get-tuple-element.12.gf_in, bf16[2,3456,128]{2,1,0:T(8,128)(2,1)S(1)} %get-tuple-element.13.gw_in), custom_call_target="tpu_custom_call" | custom-call | tf_op jit(solution)/shard_map/pallas_call | solution.py:614

commit v6 on v5

--- a/solution.py
+++ b/solution.py
@@ -131,6 +131,7 @@
     bufs_q, bufs_p = refs[56:60], refs[60:64]
     w_sem, halo_s, halo_r, core_s, core_r = refs[64:69]
     sems_q, sems_p = refs[69:79], refs[79:89]
+    early = refs[89]
     nx, ny, nzhi, nzlo, _ = dims
     nz = nzhi * nzlo
     ngx, ngy = nzlo * ny * 2, nx * nzhi
@@ -237,10 +238,10 @@
             copies.append(remote(src, dst, halo_s.at[n, m], halo_r.at[n, m], who))
 
         for d in range(2):
-            add(halo.wall_out.at[d], halo.wall.at[d, 2 + 2 * d : 4 + 2 * d], (gx, near_y[d]))
-        for d in range(2):
             for e in range(2):
                 add(halo.diag_out.at[d, e], halo.diag.at[d, e], (near_x[d], near_y[e]))
+        for d in range(2):
+            add(halo.wall_out.at[d], halo.wall.at[d, 2 + 2 * d : 4 + 2 * d], (gx, near_y[d]))
         for d in range(2):
             add(halo.face_out.at[d], halo.face.at[d, 6 + 6 * d : 8 + 6 * d], (near_x[d], gy))
         if n == 0:
@@ -453,7 +454,7 @@
                 row = (9 * a + 3 * c + e) * CH
                 if add is not None:
                     block = block + add[row : row + CH].astype(F32)
-                dst[row : row + CH] = block.astype(BF)
+                dst[row : row + CH] = block.astype(dst.dtype)
 
     core_copies = [
         remote(
@@ -465,16 +466,26 @@
         )
         for a in range(3)
     ]
-    for a in range(3):
+    weight_grad(1 - core, 0, gwo)
+    core_copies[0].start()
+    weight_grad(core, 0, early)
+    for a in range(1, 3):
         weight_grad(1 - core, a, gwo)
         core_copies[a].start()
     part_q = Part(remote, gwm, gw_ref, 0, third, line, plane, bufs_q, sems_q)
     part_p = Part(remote, gwm, gw_ref, third, 2 * third, plane, line, bufs_p, sems_p)
-    for a in range(3):
+    core_copies[0].wait()
+
+    def add_first(t, carry):
+        rows = pl.ds(pl.multiple_of(t * CH, CH), CH)
+        gwm[rows] = (early[rows] + crecv[rows].astype(F32)).astype(BF)
+        return carry
+
+    lax.fori_loop(0, 9, add_first, 0)
+    part_q.scatter_one()
+    for a in range(1, 3):
         core_copies[a].wait()
         weight_grad(core, a, gwm, crecv)
-        if a == 0:
-            part_q.scatter_one()
     part_p.scatter_one()
     inner(fb0, zb, 0)
     inner(fb1, zb, 1)
@@ -596,6 +607,7 @@
             *bufs_q, *bufs_p,
             sem(2), sem(4, 10), sem(4, 10), sem(3), sem(3),
             *sems_q, *sems_p,
+            pltpu.VMEM((rows // 3, CH), F32),
         ],
         compiler_params=pltpu.CompilerParams(
             collective_id=0, has_side_effects=True, vmem_limit_bytes=56 * 2**20

time: 64.3 us -> 63.9 us (level)
  no operation moved by 1% of the time
where the time goes in v6:
time: 63.9 us; the launch traced here: 63.8 us
  Pallas kernels  63.2 us (99%)
  between operations  0.64 us (1%)
    pallas_call x1, Pallas kernels, on_device(): pl.pallas_call(functools.partial(kernel, dims, scale), out_shape=(pltpu.V...  61.2 us
    pallas_call x1, Pallas kernels, on_device(): pl.pallas_call(convert, out_shape=(jax.ShapeDtypeStruct(features.shape, B...  2.03 us

profile of v6, /device:TPU:1, one launch (start us, length us, event | category | flops | bytes accessed | tf_op | source)
XLA Modules:
  0.0 63.8 jit_solution(5845789080050667301)
XLA Ops:
  0.6 61.2 %shard_map.120 = (bf16[2,512,128]{2,1,0:T(8,128)(2,1)S(1)}, bf16[2,512,128]{2,1,0:T(8,128)(2,1)S(1)}, bf16[2,3456,128]{2,1,0:T(8,128)(2,1)S(1)}) custom-call(bf16[2,512,128]{2,1,0:T(8,128)(2,1)} %refs_0_.1, s32[2,512]{1,0:T(2,128)} %refs_1_.1, bf16[3456,128]{1,0:T(8,128)(2,1)} %bitcast.7, f32[1,128]{1,0:T(1,128)} %bitcast.11, bf16[3456,128]{1,0:T(8,128)(2,1)} %bitcast.8, ...), custom_call_target="tpu_custom_call" | custom-call | tf_op jit(solution)/shard_map/pallas_call | solution.py:593
  61.8 2.0 %shard_map.121 = (bf16[2,512,128]{2,1,0:T(8,128)(2,1)}, bf16[2,512,128]{2,1,0:T(8,128)(2,1)}, f32[3456,128]{1,0:T(8,128)}, f32[3456,128]{1,0:T(8,128)}) custom-call(bf16[2,512,128]{2,1,0:T(8,128)(2,1)S(1)} %get-tuple-element.11.out_in, bf16[2,512,128]{2,1,0:T(8,128)(2,1)S(1)} %get-tuple-element.12.gf_in, bf16[2,3456,128]{2,1,0:T(8,128)(2,1)S(1)} %get-tuple-element.13.gw_in), custom_call_target="tpu_custom_call" | custom-call | tf_op jit(solution)/shard_map/pallas_call | solution.py:626
